TPU v7x, 32 devices: a whole 2x2x4 slice. The times are simulated.
32 devices in a mesh: seq: 8 (over z, x), hg: 4 (over y, core).
Axes of the slice: x: 2, y: 2, z: 4, core: 2. Of those that a mesh axis runs over, the one named last changes fastest.
Arguments:
- conv_input: bfloat16 [16384, 4096], P('seq', 'hg'), may hold values from -6 to 6
- grad_output: bfloat16 [16384, 4096], P('seq', 'hg'), may hold values from -0.015625 to 0.015625
- inject: bfloat16 [16384, 128], P('seq'), may hold values from -6 to 6
- readout: bfloat16 [16384, 128], P('seq'), may hold values from -6 to 6
- conv_weight: bfloat16 [4, 4096], P(None, 'hg'), may hold values from -3 to 3
- decay_codes: int32 [64, 64], P('hg', 'seq'), may hold values from 0 to 1000, as said below
Outputs:
- grad_input: float32 [16384, 4096], P('seq', 'hg')
- grad_inject: float32 [16384, 128], P('seq')
- grad_readout: float32 [16384, 128], P('seq')
Inputs may be any that keep to these rules, and one draw needn't show every extreme that they name: The decay of every step of span c in head h is 1 - 1e-6 decay_codes[h, c].
All inputs are finite; a program needn't handle non-finite values.
Results may differ from a plain program's by a relative error of at most 0.0029.
Values may be sent and summed in bfloat16 or wider, within the bound.
A program may use at most 128 MiB of HBM per device.

v0:
```python
import jax
import jax.numpy as jnp
from jax import lax
from jax.experimental import pallas as pl
from jax.experimental.pallas import tpu as pltpu
from jax.sharding import PartitionSpec as P

F32 = jnp.float32
BF16 = jnp.bfloat16
HALO = 16


def mm(a, b, ca, cb):
    return lax.dot_general(a, b, (((ca,), (cb,)), ((), ())), preferred_element_type=F32)


def chunks_of(channels):
    width = 128
    return [slice(i, i + width) for i in range(0, channels, width)]


def load_rows(first, x_ref, prev_ref, halo_ref, xs):
    span = x_ref.shape[0]

    @pl.when(first)
    def _():
        xs[0:HALO] = halo_ref[...].astype(F32)

    @pl.when(jnp.logical_not(first))
    def _():
        xs[0:HALO] = prev_ref[...].astype(F32)

    xs[HALO : HALO + span] = x_ref[...].astype(F32)


def preact_of(xs, w_ref, cols, span):
    v = w_ref[0:1, cols] * xs[HALO - 3 : HALO - 3 + span, cols]
    for k in range(1, 4):
        v = v + w_ref[k : k + 1, cols] * xs[HALO - 3 + k : HALO - 3 + k + span, cols]
    return v


def centred(span, width):
    rows = lax.broadcasted_iota(jnp.int32, (span, width), 0)
    return (rows - span // 2).astype(F32)


def fold_kernel(
    x_ref, prev_ref, halo_ref, g_ref, b_ref, c_ref, w_ref, lr_ref,
    before_ref, fresh_ref, own_state_ref, own_grad_ref,
    xs, act, da, dg, running,
):
    s = pl.program_id(0)
    span, channels = x_ref.shape
    load_rows(s == 0, x_ref, prev_ref, halo_ref, xs)

    @pl.when(s == 0)
    def _():
        own_state_ref[...] = jnp.zeros_like(own_state_ref)
        own_grad_ref[...] = jnp.zeros_like(own_grad_ref)
        running[...] = jnp.zeros_like(running)

    for cols in chunks_of(channels):
        v = preact_of(xs, w_ref, cols, span)
        a = (v * (1.0 / (1.0 + jnp.exp(-v)))).astype(BF16)
        act[:, cols] = a
        turn = centred(span, a.shape[1]) * lr_ref[0, 0:1, cols]
        da[:, cols] = (a.astype(F32) * (jnp.exp(-turn) - 1.0)).astype(BF16)
        dg[:, cols] = (g_ref[:, cols].astype(F32) * (jnp.exp(turn) - 1.0)).astype(BF16)
    lr = lr_ref[0]
    half = span // 2
    b, c = b_ref[...], c_ref[...]
    fresh_state = jnp.exp((half - 1.0) * lr) * (mm(b, act[...], 0, 0) + mm(b, da[...], 0, 0))
    fresh_grad = jnp.exp((half + 1.0) * lr) * (mm(c, g_ref[...], 0, 0) + mm(c, dg[...], 0, 0))
    before_ref[0] = own_state_ref[...]
    fresh_ref[0] = fresh_grad
    own_state_ref[...] = jnp.exp(span * lr) * own_state_ref[...] + fresh_state
    own_grad_ref[...] = own_grad_ref[...] + jnp.exp(running[0:1]) * fresh_grad
    running[...] = running[...] + span * lr


def grads_kernel(
    x_ref, prev_ref, halo_ref, g_ref, b_ref, c_ref, w_ref, lr_ref, prior_ref,
    before_ref, fresh_ref, entering_ref, arriving_ref,
    gx_ref, gb_ref, gc_ref, first_ref,
    xs, act, ab, gs, da, dg, sb_hi, sb_lo, ga_hi, ga_lo, gp, carry,
):
    t = pl.program_id(0)
    spans = pl.num_programs(0)
    span, channels = x_ref.shape
    half = span // 2
    load_rows(t == spans - 1, x_ref, prev_ref, halo_ref, xs)

    @pl.when(t == 0)
    def _():
        carry[...] = arriving_ref[...]
        gp[span : span + 8] = jnp.zeros((8, channels), F32)

    @pl.when(t > 0)
    def _():
        gp[span : span + 8] = gp[0:8]

    for cols in chunks_of(channels):
        lr = lr_ref[0, 0:1, cols]
        v = preact_of(xs, w_ref, cols, span)
        a = (v * (1.0 / (1.0 + jnp.exp(-v)))).astype(BF16)
        act[:, cols] = a
        turn = centred(span, a.shape[1]) * lr
        af = a.astype(F32)
        a_more = af * (jnp.exp(-turn) - 1.0)
        ab[:, cols] = (af + a_more).astype(BF16)
        da[:, cols] = a_more.astype(BF16)
        gf = g_ref[:, cols].astype(F32)
        g_more = gf * (jnp.exp(turn) - 1.0)
        gs[:, cols] = (gf + g_more).astype(BF16)
        dg[:, cols] = g_more.astype(BF16)
        held = carry[:, cols]
        sb = jnp.exp((half + 1.0) * lr) * (
            before_ref[0, :, cols] + prior_ref[0, 0:1, cols] * entering_ref[:, cols]
        )
        hi = sb.astype(BF16)
        sb_hi[:, cols] = hi
        sb_lo[:, cols] = (sb - hi.astype(F32)).astype(BF16)
        ga = jnp.exp((half - 1.0) * lr) * held
        hi = ga.astype(BF16)
        ga_hi[:, cols] = hi
        ga_lo[:, cols] = (ga - hi.astype(F32)).astype(BF16)
        carry[:, cols] = jnp.exp(span * lr) * held + fresh_ref[0, :, cols]

    b, c = b_ref[...], c_ref[...]
    rows = lax.broadcasted_iota(jnp.int32, (span, span), 0)
    columns = lax.broadcasted_iota(jnp.int32, (span, span), 1)
    lower = rows >= columns
    pairs = jnp.where(lower, mm(gs[...], ab[...], 1, 1), 0.0).astype(BF16)
    gb_ref[...] = (
        mm(pairs, c, 0, 0)
        + mm(act[...], ga_hi[...], 1, 1)
        + mm(act[...], ga_lo[...], 1, 1)
        + mm(da[...], ga_hi[...], 1, 1)
    )
    gc_ref[...] = (
        mm(pairs, b, 1, 0)
        + mm(g_ref[...], sb_hi[...], 1, 1)
        + mm(g_ref[...], sb_lo[...], 1, 1)
        + mm(dg[...], sb_hi[...], 1, 1)
    )
    mixed = jnp.where(lower, mm(c, b, 1, 1), 0.0).astype(BF16)

    for cols in chunks_of(channels):
        grad_act = mm(mixed, gs[:, cols], 0, 0) + mm(b, ga_hi[:, cols], 1, 0)
        grad_act = grad_act + mm(b, ga_lo[:, cols], 1, 0)
        v = preact_of(xs, w_ref, cols, span)
        squashed = 1.0 / (1.0 + jnp.exp(-v))
        slope = squashed * (1.0 + v * (1.0 - squashed))
        turn = centred(span, v.shape[1]) * lr_ref[0, 0:1, cols]
        gp[0:span, cols] = grad_act * jnp.exp(-turn) * slope
        out = w_ref[0:1, cols] * gp[3 : 3 + span, cols]
        for k in range(1, 4):
            out = out + w_ref[k : k + 1, cols] * gp[3 - k : 3 - k + span, cols]
        gx_ref[:, cols] = out
    first_ref[...] = gp[0:8]


def shifted(array, axis, by):
    length = lax.axis_size(axis)
    return lax.ppermute(
        array, axis, [(i, i + by) for i in range(length) if 0 <= i + by < length]
    )


def swapped(array, axis, flip):
    return lax.ppermute(array, axis, [(i, i ^ flip) for i in range(lax.axis_size(axis))])


def across_devices(own_state, own_grad, logs, head_dim):
    length, me = lax.axis_size("seq"), lax.axis_index("seq")
    places = jnp.arange(length)

    def gain(low, high):
        held = jnp.where(((places >= low) & (places <= high))[:, None], logs, 0.0)
        return jnp.repeat(jnp.exp(jnp.sum(held, axis=0)), head_dim)[None, :]

    entering, arriving = jnp.zeros_like(own_state), jnp.zeros_like(own_grad)
    state, grad = own_state, own_grad
    step = 1
    while step < length:
        got_state = shifted(state.astype(BF16), "seq", step).astype(F32)
        got_grad = shifted(grad.astype(BF16), "seq", -step).astype(F32)
        entering = entering + gain(me - step + 1, me - 1) * got_state
        arriving = arriving + gain(me + 1, me + step - 1) * got_grad
        if 2 * step < length:
            state = state + gain(me - step + 1, me) * got_state
            grad = grad + gain(me, me + step - 1) * got_grad
        step *= 2
    return entering, arriving


def summed_over_groups(both):
    length = lax.axis_size("hg")
    rows = both.shape[0] // 2
    odd = (lax.axis_index("hg") % 2) == 1
    low, high = both[:rows], both[rows:]
    mine = jnp.where(odd, high, low) + swapped(jnp.where(odd, low, high), "hg", 1)
    flip = 2
    while flip < length:
        sent = mine.astype(BF16)
        mine = sent.astype(F32) + swapped(sent, "hg", flip).astype(F32)
        flip *= 2
    other = swapped(mine, "hg", 1)
    return jnp.concatenate([jnp.where(odd, other, mine), jnp.where(odd, mine, other)], axis=0)


def body(conv_input, grad_output, inject, readout, conv_weight, decay_codes):
    tokens, channels = conv_input.shape
    heads, spans = decay_codes.shape
    span = tokens // spans
    head_dim = channels // heads
    states = inject.shape[1]
    weights = conv_weight.astype(F32)
    log_rates = jnp.log1p(-decay_codes.astype(F32) * 1e-06)
    own_logs = span * jnp.sum(log_rates, axis=1)
    logs = lax.all_gather(own_logs, "seq", axis=0)
    halo = shifted(conv_input[tokens - HALO :], "seq", 1)
    wide = jnp.repeat(log_rates.T, head_dim, axis=1)
    prior = jnp.exp(span * (jnp.cumsum(wide, axis=0) - wide))[:, None]
    lr = wide[:, None]
    step = span // HALO

    def specs(at):
        return [
            pl.BlockSpec((span, channels), lambda t: (at(t), 0)),
            pl.BlockSpec((HALO, channels), lambda t: (jnp.maximum(at(t) * step - 1, 0), 0)),
            pl.BlockSpec((HALO, channels), lambda t: (0, 0)),
            pl.BlockSpec((span, channels), lambda t: (at(t), 0)),
            pl.BlockSpec((span, states), lambda t: (at(t), 0)),
            pl.BlockSpec((span, states), lambda t: (at(t), 0)),
            pl.BlockSpec((4, channels), lambda t: (0, 0)),
            pl.BlockSpec((1, 1, channels), lambda t: (at(t), 0, 0)),
        ]

    per_span = jax.ShapeDtypeStruct((spans, states, channels), F32)
    one = jax.ShapeDtypeStruct((states, channels), F32)
    params = pltpu.CompilerParams(
        vmem_limit_bytes=48 << 20, dimension_semantics=("arbitrary",)
    )
    whole = pl.BlockSpec((states, channels), lambda t: (0, 0))
    lines = pltpu.VMEM((span + HALO, channels), F32)
    tile = pltpu.VMEM((span, channels), BF16)
    before, fresh, own_state, own_grad = pl.pallas_call(
        fold_kernel,
        grid=(spans,),
        in_specs=specs(lambda t: t),
        out_specs=[pl.BlockSpec((1, states, channels), lambda t: (t, 0, 0))] * 2 + [whole] * 2,
        out_shape=[per_span, per_span, one, one],
        scratch_shapes=[lines, tile, tile, tile, pltpu.VMEM((8, channels), F32)],
        compiler_params=params,
        name="fold",
    )(conv_input, conv_input, halo, grad_output, inject, readout, weights, lr)

    entering, arriving = across_devices(own_state, own_grad, logs, head_dim)

    back = lambda t: spans - 1 - t
    state_tile = pltpu.VMEM((states, channels), BF16)
    grad_input, grad_inject, grad_readout, first = pl.pallas_call(
        grads_kernel,
        grid=(spans,),
        in_specs=specs(back)
        + [pl.BlockSpec((1, 1, channels), lambda t: (back(t), 0, 0))]
        + [pl.BlockSpec((1, states, channels), lambda t: (back(t), 0, 0))] * 2
        + [whole] * 2,
        out_specs=[
            pl.BlockSpec((span, channels), lambda t: (back(t), 0)),
            pl.BlockSpec((span, states), lambda t: (back(t), 0)),
            pl.BlockSpec((span, states), lambda t: (back(t), 0)),
            pl.BlockSpec((8, channels), lambda t: (0, 0)),
        ],
        out_shape=[
            jax.ShapeDtypeStruct((tokens, channels), F32),
            jax.ShapeDtypeStruct((tokens, states), F32),
            jax.ShapeDtypeStruct((tokens, states), F32),
            jax.ShapeDtypeStruct((8, channels), F32),
        ],
        scratch_shapes=[lines]
        + [tile] * 5
        + [state_tile] * 4
        + [pltpu.VMEM((span + 8, channels), F32), pltpu.VMEM((states, channels), F32)],
        compiler_params=params,
        name="grads",
    )(
        conv_input, conv_input, halo, grad_output, inject, readout, weights, lr, prior,
        before, fresh, entering, arriving,
    )
    later = shifted(first, "seq", -1)
    edge = jnp.stack(
        [sum(weights[k] * later[r - k] for k in range(r + 1)) for r in range(3)], axis=0
    )
    last = grad_input[tokens - 8 :] + jnp.pad(edge, ((5, 0), (0, 0)))
    grad_input = lax.dynamic_update_slice(grad_input, last, (tokens - 8, 0))
    both = summed_over_groups(jnp.concatenate([grad_inject, grad_readout], axis=1))
    return grad_input, both[:, :states], both[:, states:]


def solution(mesh):
    return jax.shard_map(
        body,
        mesh=mesh,
        in_specs=(
            P("seq", "hg"),
            P("seq", "hg"),
            P("seq", None),
            P("seq", None),
            P(None, "hg"),
            P("hg", "seq"),
        ),
        out_specs=(P("seq", "hg"), P("seq", None), P("seq", None)),
        check_vma=False,
    )
```

profile of v0, /device:TPU:0, one launch (start us, length us, event | category | flops | bytes accessed | tf_op | source)
XLA Modules:
  0.0 163.4 jit_solution(17600117504124049082)
XLA Ops:
  0.6 0.8 slice.42
  1.4 4.8 %collective-permute-start = (bf16[16,1024]{1,0:T(8,128)(2,1)S(1)}, bf16[16,1024]{1,0:T(8,128)(2,1)S(1)}, u32[]{:S(2)}, u32[]{:S(2)}) collective-permute-start(bf16[16,1024]{1,0:T(8,128)(2,1)S(1)} %slice.42), channel_id=1, source_target_pairs={{0,4},{4,8},{8,12},{12,16},{16,20},{20,24},{24,28},{1,5},{5,9},{9,... | collective-permute-start | bytes 98312 | tf_op jit(solution)/shard_map/ppermute | solution.py:166
  6.3 0.7 fusion.19
  7.0 1.2 dynamic-slice
  9.0 0.7 convert_element_type.53.w_ref
  9.9 1.0 copy-done
  10.9 1.0 copy-done.2
  12.0 23.5 %fold.1 = (f32[8,128,1024]{2,1,0:T(8,128)}, f32[8,128,1024]{2,1,0:T(8,128)}, f32[128,1024]{1,0:T(8,128)S(1)}, f32[128,1024]{1,0:T(8,128)S(1)}) custom-call(bf16[2048,1024]{1,0:T(8,128)(2,1)} %prev_ref.3, bf16[2048,1024]{1,0:T(8,128)(2,1)} %prev_ref.3, bf16[16,1024]{1,0:T(8,128)(2,1)S(1)} %collective-permute-done.halo_ref, bf16[2048,1024]{1,0:T(8,128)(2,1)} %g_ref.3, ...), custom_call_target="tpu_custom_call" | custom-call | tf_op jit(solution)/shard_map/fold/pallas_call | solution.py:249
  35.5 1.3 collective-permute-start.4
  36.8 4.6 %collective-permute-start.1 = (bf16[128,1024]{1,0:T(8,128)(2,1)S(1)}, bf16[128,1024]{1,0:T(8,128)(2,1)S(1)}, u32[]{:S(2)}, u32[]{:S(2)}) collective-permute-start(bf16[128,1024]{1,0:T(8,128)(2,1)S(1)} %convert_element_type.55), channel_id=1, source_target_pairs={{0,4},{4,8},{8,12},{12,16},{16,20},{20,24},{24,28},{1,5},{5,9},{9,... | collective-permute-start | bytes 786440 | tf_op jit(solution)/shard_map/ppermute | solution.py:166
  41.4 21.8 %all-reduce.1 = f32[128]{0:T(128)S(1)} all-reduce(f32[128]{0:T(128)S(1)} %multiply_dynamic-update-slice_fusion), channel_id=2, replica_groups=mesh['seq'=8,'hg'=4] {'seq'}, use_global_device_ids=true, to_apply=%add.1 | all-reduce | flops 128 | bytes 1024
  63.6 0.2 fusion.13
  63.7 1.3 collective-permute-start.5
  65.0 4.6 %collective-permute-start.2 = (bf16[128,1024]{1,0:T(8,128)(2,1)S(1)}, bf16[128,1024]{1,0:T(8,128)(2,1)S(1)}, u32[]{:S(2)}, u32[]{:S(2)}) collective-permute-start(bf16[128,1024]{1,0:T(8,128)(2,1)S(1)} %get-tuple-element.38), channel_id=1, source_target_pairs={{0,8},{4,12},{8,16},{12,20},{16,24},{20,28},{1,9},{5,13},{9,17},{1... | collective-permute-start | bytes 786440 | tf_op jit(solution)/shard_map/ppermute | solution.py:166
  69.9 2.1 %collective-permute-done.5 = bf16[128,1024]{1,0:T(8,128)(2,1)S(1)} collective-permute-done((bf16[128,1024]{1,0:T(8,128)(2,1)S(1)}, bf16[128,1024]{1,0:T(8,128)(2,1)S(1)}, u32[]{:S(2)}, u32[]{:S(2)}) %collective-permute-start.5) | collective-permute-done | bytes 262176 | tf_op jit(solution)/shard_map/ppermute | solution.py:166
  72.0 1.5 collective-permute-done.2
  73.5 0.3 fusion.12
  73.8 1.4 collective-permute-start.6
  75.2 5.5 %collective-permute-start.3 = (bf16[128,1024]{1,0:T(8,128)(2,1)S(1)}, bf16[128,1024]{1,0:T(8,128)(2,1)S(1)}, u32[]{:S(2)}, u32[]{:S(2)}) collective-permute-start(bf16[128,1024]{1,0:T(8,128)(2,1)S(1)} %get-tuple-element.36), channel_id=1, source_target_pairs={{0,16},{4,20},{8,24},{12,28},{1,17},{5,21},{9,25},{13,29},{2,18},{... | collective-permute-start | bytes 786440 | tf_op jit(solution)/shard_map/ppermute | solution.py:166
  81.7 5.1 %collective-permute-done.6 = bf16[128,1024]{1,0:T(8,128)(2,1)S(1)} collective-permute-done((bf16[128,1024]{1,0:T(8,128)(2,1)S(1)}, bf16[128,1024]{1,0:T(8,128)(2,1)S(1)}, u32[]{:S(2)}, u32[]{:S(2)}) %collective-permute-start.6) | collective-permute-done | bytes 262176 | tf_op jit(solution)/shard_map/ppermute | solution.py:166
  86.7 0.1 fusion.9.arriving_ref
  86.9 0.1 fusion.4.entering_ref
  87.1 49.9 %grads.1 = (f32[2048,1024]{1,0:T(8,128)}, f32[2048,128]{1,0:T(8,128)S(1)}, f32[2048,128]{1,0:T(8,128)S(1)}, f32[8,1024]{1,0:T(8,128)S(1)}) custom-call(bf16[2048,1024]{1,0:T(8,128)(2,1)} %prev_ref.3, bf16[2048,1024]{1,0:T(8,128)(2,1)} %prev_ref.3, bf16[16,1024]{1,0:T(8,128)(2,1)S(1)} %collective-permute-done.halo_ref, bf16[2048,1024]{1,0:T(8,128)(2,1)} %g_ref.3, ...), custom_call_target="tpu_custom_call" | custom-call | tf_op jit(solution)/shard_map/grads/pallas_call | solution.py:264
  137.4 2.6 %collective-permute-done.8 = f32[1024,256]{1,0:T(8,128)S(1)} collective-permute-done((f32[1024,256]{1,0:T(8,128)S(1)}, f32[1024,256]{1,0:T(8,128)S(1)}, u32[]{:S(2)}, u32[]{:S(2)}) %collective-permute-start.8) | collective-permute-done | bytes 1048608 | tf_op jit(solution)/shard_map/ppermute | solution.py:172
  140.1 0.2 add_convert_fusion
  140.3 1.6 collective-permute-start.9
  141.9 12.4 %collective-permute-done.9 = bf16[1024,256]{1,0:T(8,128)(2,1)S(1)} collective-permute-done((bf16[1024,256]{1,0:T(8,128)(2,1)S(1)}, bf16[1024,256]{1,0:T(8,128)(2,1)S(1)}, u32[]{:S(2)}, u32[]{:S(2)}) %collective-permute-start.9) | collective-permute-done | bytes 524320 | tf_op jit(solution)/shard_map/ppermute | solution.py:172
  154.5 1.3 collective-permute-start.7
  155.8 4.5 %collective-permute-done.7 = f32[8,1024]{1,0:T(8,128)S(1)} collective-permute-done((f32[8,1024]{1,0:T(8,128)S(1)}, f32[8,1024]{1,0:T(8,128)S(1)}, u32[]{:S(2)}, u32[]{:S(2)}) %collective-permute-start.7) | collective-permute-done | bytes 32800 | tf_op jit(solution)/shard_map/ppermute | solution.py:166
  160.4 1.4 fusion.16
  161.8 0.2 broadcast_select_fusion
  162.0 1.5 pad_maximum_fusion
  (59 shorter events, 2.6 us)
Async XLA Ops:
  1.4 8.5 %collective-permute-start = (bf16[16,1024]{1,0:T(8,128)(2,1)S(1)}, bf16[16,1024]{1,0:T(8,128)(2,1)S(1)}, u32[]{:S(2)}, u32[]{:S(2)}) collective-permute-start(bf16[16,1024]{1,0:T(8,128)(2,1)S(1)} %slice.42), channel_id=1, source_target_pairs={{0,4},{4,8},{8,12},{12,16},{16,20},{20,24},{24,28},{1,5},{5,9},{9,... | collective-permute-start | bytes 98312 | tf_op jit(solution)/shard_map/ppermute | solution.py:166
  9.9 1.0 copy-start
  10.9 1.0 copy-start.2
  35.5 28.0 %collective-permute-start.4 = (bf16[128,1024]{1,0:T(8,128)(2,1)S(1)}, bf16[128,1024]{1,0:T(8,128)(2,1)S(1)}, u32[]{:S(2)}, u32[]{:S(2)}) collective-permute-start(bf16[128,1024]{1,0:T(8,128)(2,1)S(1)} %convert_element_type.61), channel_id=1, source_target_pairs={{4,0},{8,4},{12,8},{16,12},{20,16},{24,20},{28,24},{5,1},{9,5},{13... | collective-permute-start | bytes 786440 | tf_op jit(solution)/shard_map/ppermute | solution.py:166
  36.8 26.7 %collective-permute-start.1 = (bf16[128,1024]{1,0:T(8,128)(2,1)S(1)}, bf16[128,1024]{1,0:T(8,128)(2,1)S(1)}, u32[]{:S(2)}, u32[]{:S(2)}) collective-permute-start(bf16[128,1024]{1,0:T(8,128)(2,1)S(1)} %convert_element_type.55), channel_id=1, source_target_pairs={{0,4},{4,8},{8,12},{12,16},{16,20},{20,24},{24,28},{1,5},{5,9},{9,... | collective-permute-start | bytes 786440 | tf_op jit(solution)/shard_map/ppermute | solution.py:166
  63.7 8.3 %collective-permute-start.5 = (bf16[128,1024]{1,0:T(8,128)(2,1)S(1)}, bf16[128,1024]{1,0:T(8,128)(2,1)S(1)}, u32[]{:S(2)}, u32[]{:S(2)}) collective-permute-start(bf16[128,1024]{1,0:T(8,128)(2,1)S(1)} %get-tuple-element.37), channel_id=1, source_target_pairs={{8,0},{12,4},{16,8},{20,12},{24,16},{28,20},{9,1},{13,5},{17,9},{2... | collective-permute-start | bytes 786440 | tf_op jit(solution)/shard_map/ppermute | solution.py:166
  65.0 8.4 %collective-permute-start.2 = (bf16[128,1024]{1,0:T(8,128)(2,1)S(1)}, bf16[128,1024]{1,0:T(8,128)(2,1)S(1)}, u32[]{:S(2)}, u32[]{:S(2)}) collective-permute-start(bf16[128,1024]{1,0:T(8,128)(2,1)S(1)} %get-tuple-element.38), channel_id=1, source_target_pairs={{0,8},{4,12},{8,16},{12,20},{16,24},{20,28},{1,9},{5,13},{9,17},{1... | collective-permute-start | bytes 786440 | tf_op jit(solution)/shard_map/ppermute | solution.py:166
  73.7 13.3 %copy-start.1 = (bf16[2048,128]{1,0:T(8,128)(2,1)S(1)}, bf16[2048,128]{1,0:T(8,128)(2,1)}, u32[]{:S(2)}) copy-start(bf16[2048,128]{1,0:T(8,128)(2,1)} %b_ref.3) | copy-start | bytes 1572868
  73.7 13.3 %copy-start.3 = (bf16[2048,128]{1,0:T(8,128)(2,1)S(1)}, bf16[2048,128]{1,0:T(8,128)(2,1)}, u32[]{:S(2)}) copy-start(bf16[2048,128]{1,0:T(8,128)(2,1)} %c_ref.3) | copy-start | bytes 1572868
  73.8 13.0 %collective-permute-start.6 = (bf16[128,1024]{1,0:T(8,128)(2,1)S(1)}, bf16[128,1024]{1,0:T(8,128)(2,1)S(1)}, u32[]{:S(2)}, u32[]{:S(2)}) collective-permute-start(bf16[128,1024]{1,0:T(8,128)(2,1)S(1)} %get-tuple-element.35), channel_id=1, source_target_pairs={{16,0},{20,4},{24,8},{28,12},{17,1},{21,5},{25,9},{29,13},{18,2},{... | collective-permute-start | bytes 786440 | tf_op jit(solution)/shard_map/ppermute | solution.py:166
  75.2 11.7 %collective-permute-start.3 = (bf16[128,1024]{1,0:T(8,128)(2,1)S(1)}, bf16[128,1024]{1,0:T(8,128)(2,1)S(1)}, u32[]{:S(2)}, u32[]{:S(2)}) collective-permute-start(bf16[128,1024]{1,0:T(8,128)(2,1)S(1)} %get-tuple-element.36), channel_id=1, source_target_pairs={{0,16},{4,20},{8,24},{12,28},{1,17},{5,21},{9,25},{13,29},{2,18},{... | collective-permute-start | bytes 786440 | tf_op jit(solution)/shard_map/ppermute | solution.py:166
  137.3 2.7 %collective-permute-start.8 = (f32[1024,256]{1,0:T(8,128)S(1)}, f32[1024,256]{1,0:T(8,128)S(1)}, u32[]{:S(2)}, u32[]{:S(2)}) collective-permute-start(f32[1024,256]{1,0:T(8,128)S(1)} %slice_select_fusion), channel_id=1, source_target_pairs={{0,1},{1,0},{2,3},{3,2},{4,5},{5,4},{6,7},{7,6},{8,9},{9,8},{10,11... | collective-permute-start | bytes 3145736 | tf_op jit(solution)/shard_map/ppermute | solution.py:172
  140.3 14.0 %collective-permute-start.9 = (bf16[1024,256]{1,0:T(8,128)(2,1)S(1)}, bf16[1024,256]{1,0:T(8,128)(2,1)S(1)}, u32[]{:S(2)}, u32[]{:S(2)}) collective-permute-start(bf16[1024,256]{1,0:T(8,128)(2,1)S(1)} %add_convert_fusion), channel_id=1, source_target_pairs={{0,2},{1,3},{2,0},{3,1},{4,6},{5,7},{6,4},{7,5},{8,10},{9,11},{10,... | collective-permute-start | bytes 1572872 | tf_op jit(solution)/shard_map/ppermute | solution.py:172
  154.5 7.3 %collective-permute-start.10 = (f32[1024,256]{1,0:T(8,128)S(1)}, f32[1024,256]{1,0:T(8,128)S(1)}, u32[]{:S(2)}, u32[]{:S(2)}) collective-permute-start(f32[1024,256]{1,0:T(8,128)S(1)} %convert_add_fusion), channel_id=1, source_target_pairs={{0,1},{1,0},{2,3},{3,2},{4,5},{5,4},{6,7},{7,6},{8,9},{9,8},{10,11... | collective-permute-start | bytes 3145736 | tf_op jit(solution)/shard_map/ppermute | solution.py:172
  154.5 5.8 %collective-permute-start.7 = (f32[8,1024]{1,0:T(8,128)S(1)}, f32[8,1024]{1,0:T(8,128)S(1)}, u32[]{:S(2)}, u32[]{:S(2)}) collective-permute-start(f32[8,1024]{1,0:T(8,128)S(1)} %get-tuple-element.16), channel_id=1, source_target_pairs={{4,0},{8,4},{12,8},{16,12},{20,16},{24,20},{28,24},{5,1},{9,5},{13... | collective-permute-start | bytes 98312 | tf_op jit(solution)/shard_map/ppermute | solution.py:166
where the time goes:
time: 164 us; the launch traced here: 163 us
  Pallas kernels  73.4 us (45%)
  waiting for transfers between devices  28.2 us (17%)
  starting transfers between devices  26.5 us (16%)
  blocking collectives  21.8 us (13%)
  other arithmetic  6.04 us (4%)
  local copies, waits for them, and re-layouts  5.84 us (4%)
  between operations  1.65 us (1%)
    pallas_call x1, Pallas kernels, body(): pl.pallas_call(grads_kernel, grid=(spans,), in_specs=specs(back) + [pl.Bl...  49.9 us
    ppermute x8, starting transfers between devices, shifted(): lax.ppermute(array, axis, [(i, i + by) for i in range(length) if 0 <= i +...  24.7 us
    pallas_call x1, Pallas kernels, body(): pl.pallas_call(fold_kernel, grid=(spans,), in_specs=specs(lambda t: t), o...  23.5 us
    unnamed x1, blocking collectives  21.8 us
    ppermute x3, waiting for transfers between devices, swapped(): lax.ppermute(array, axis, [(i, i ^ flip) for i in range(lax.axis_size(axi...  15.1 us
    ppermute x8, waiting for transfers between devices, shifted(): lax.ppermute(array, axis, [(i, i + by) for i in range(length) if 0 <= i +...  13.1 us
    unnamed x11, local copies, waits for them, and re-layouts  3.41 us
  transfers between devices with their start and end apart: 11, of which 6 were waited for; matrix products, arithmetic and copies ran while one was open for 4% of the time, Pallas kernels for 0%

commit v1 on v0

v1 whole, which is shorter than its diff:
```python
import functools

import jax
import jax.numpy as jnp
from jax import lax
from jax.experimental import pallas as pl
from jax.experimental.pallas import tpu as pltpu
from jax.sharding import PartitionSpec as P

F32 = jnp.float32
BF16 = jnp.bfloat16
HALO = 16


def mm(a, b, ca, cb):
    return lax.dot_general(a, b, (((ca,), (cb,)), ((), ())), preferred_element_type=F32)


def chunks_of(channels):
    width = 256
    return [slice(i, i + width) for i in range(0, channels, width)]


def load_rows(first, x_ref, prev_ref, halo_ref, xs):
    span = x_ref.shape[0]

    @pl.when(first)
    def _():
        xs[0:HALO] = halo_ref[...].astype(F32)

    @pl.when(jnp.logical_not(first))
    def _():
        xs[0:HALO] = prev_ref[...].astype(F32)

    xs[HALO : HALO + span] = x_ref[...].astype(F32)


def preact_of(xs, w_ref, cols, span):
    v = w_ref[0:1, cols] * xs[HALO - 3 : HALO - 3 + span, cols]
    for k in range(1, 4):
        v = v + w_ref[k : k + 1, cols] * xs[HALO - 3 + k : HALO - 3 + k + span, cols]
    return v


def decays(lr, span):
    width = lr.shape[1]
    rows = lax.broadcasted_iota(jnp.int32, (8, width), 0)
    held = jnp.exp((rows - span // 2).astype(F32) * lr)
    length = 8
    while length < span:
        held = jnp.concatenate([held, held * jnp.exp(length * lr)], axis=0)
        length *= 2
    return held


def fold_kernel(
    x_ref, prev_ref, halo_ref, g_ref, b_ref, c_ref, w_ref, lr_ref,
    act_ref, da_ref, dg_ref, slope_ref, before_ref, fresh_ref, own_state_ref, own_grad_ref,
    xs, running,
):
    s = pl.program_id(0)
    span, channels = x_ref.shape
    half = span // 2
    load_rows(s == 0, x_ref, prev_ref, halo_ref, xs)

    @pl.when(s == 0)
    def _():
        own_state_ref[...] = jnp.zeros_like(own_state_ref)
        own_grad_ref[...] = jnp.zeros_like(own_grad_ref)
        running[...] = jnp.zeros_like(running)

    b, c = b_ref[...].T, c_ref[...].T
    for cols in chunks_of(channels):
        lr = lr_ref[0, 0:1, cols]
        v = preact_of(xs, w_ref, cols, span)
        squashed = 0.5 + 0.5 * jnp.tanh(0.5 * v)
        full = v * squashed
        slope_ref[:, cols] = (squashed + full * (1.0 - squashed) - 0.5).astype(BF16)
        a = full.astype(BF16)
        act_ref[:, cols] = a
        da = (a.astype(F32) * (decays(-lr, span) - 1.0)).astype(BF16)
        da_ref[:, cols] = da
        g = g_ref[:, cols]
        dg = (g.astype(F32) * (decays(lr, span) - 1.0)).astype(BF16)
        dg_ref[:, cols] = dg
        fresh_state = jnp.exp((half - 1.0) * lr) * (mm(b, a, 1, 0) + mm(b, da, 1, 0))
        fresh_grad = jnp.exp((half + 1.0) * lr) * (mm(c, g, 1, 0) + mm(c, dg, 1, 0))
        held = own_state_ref[:, cols]
        before_ref[0, :, cols] = held
        fresh_ref[0, :, cols] = fresh_grad
        own_state_ref[:, cols] = jnp.exp(span * lr) * held + fresh_state
        own_grad_ref[:, cols] = own_grad_ref[:, cols] + jnp.exp(running[0:1, cols]) * fresh_grad
    running[...] = running[...] + span * lr_ref[0]


def log_rows(log):
    high = log.astype(BF16).astype(F32)
    mid = (log - high).astype(BF16).astype(F32)
    low = log - high - mid
    rows = lax.broadcasted_iota(jnp.int32, (HALO, log.shape[1]), 0)
    tile = jnp.where(rows == 0, high, jnp.where(rows == 1, mid, jnp.where(rows == 2, low, 0.0)))
    return tile.astype(BF16)


def inner_kernel(
    length, rounds, axis,
    g_ref, dg_ref, act_ref, da_ref, b_ref, c_ref, own_state_ref, own_grad_ref, log_ref,
    ga_ref, gb_ref, gc_ref, entering_ref, arriving_ref,
    sent, landed, held, logs, send_sem, recv_sem,
):
    t = pl.program_id(0)
    spans = pl.num_programs(0)
    span = b_ref.shape[0]
    size = own_state_ref.shape[0]
    me = lax.axis_index(axis)
    founds = (entering_ref, arriving_ref)

    def inside(device):
        return jnp.logical_and(device >= 0, device < length)

    def copy(way, r):
        by = (1 << r) * (1 - 2 * way)
        move = pltpu.make_async_remote_copy(
            src_ref=sent.at[way, r],
            dst_ref=landed.at[way, r],
            send_sem=send_sem.at[way, r],
            recv_sem=recv_sem.at[way, r],
            device_id={axis: me + by},
            device_id_type=pl.DeviceIdType.MESH,
        )
        return move, inside(me + by), inside(me - by)

    def start(r):
        for way in range(2):
            sent[way, r, 0:size] = held[way].astype(BF16)
            sent[way, r, size : size + HALO] = log_rows(logs[way, 0:1])
            move, sends, _ = copy(way, r)

            @pl.when(sends)
            def _():
                move.start()

    def finish(r):
        for way in range(2):
            move, sends, takes = copy(way, r)

            @pl.when(takes)
            def _():
                move.wait_recv()
                got = landed[way, r, 0:size].astype(F32)
                tail = landed[way, r, size : size + HALO].astype(F32)
                got_log = (tail[0:1] + tail[1:2]) + tail[2:3]
                found = founds[way]
                found[...] = found[...] + jnp.exp(logs[way, 1:2]) * got
                if r < rounds - 1:
                    held[way] = held[way] + jnp.exp(logs[way, 0:1]) * got
                    logs[way, 0:1] = logs[way, 0:1] + got_log
                    logs[way, 1:2] = logs[way, 1:2] + got_log

            @pl.when(sends)
            def _():
                move.wait_send()

    @pl.when(t == 0)
    def _():
        barrier = pltpu.get_barrier_semaphore()
        others = [me + sign * (1 << r) for r in range(rounds) for sign in (1, -1)]
        for other in others:

            @pl.when(inside(other))
            def _():
                pl.semaphore_signal(
                    barrier, inc=1, device_id={axis: other}, device_id_type=pl.DeviceIdType.MESH
                )

        pl.semaphore_wait(barrier, sum(jnp.where(inside(other), 1, 0) for other in others))

        for way, (own, found) in enumerate(zip((own_state_ref, own_grad_ref), founds)):
            held[way] = own[...]
            logs[way, 0:1] = log_ref[...]
            logs[way, 1:2] = jnp.zeros_like(log_ref)
            found[...] = jnp.zeros_like(found)

    for r in range(rounds):

        @pl.when(t == r * spans // rounds)
        def _():
            if r > 0:
                finish(r - 1)
            start(r)

    b, c = b_ref[...], c_ref[...]
    rows = lax.broadcasted_iota(jnp.int32, (span, span), 0)
    columns = lax.broadcasted_iota(jnp.int32, (span, span), 1)
    mixed = jnp.where(rows <= columns, mm(b, c, 1, 1), 0.0).astype(BF16)
    pairs = jnp.zeros((span, span), F32)
    for cols in chunks_of(g_ref.shape[1]):
        gs = (g_ref[:, cols].astype(F32) + dg_ref[:, cols].astype(F32)).astype(BF16)
        ab = (act_ref[:, cols].astype(F32) + da_ref[:, cols].astype(F32)).astype(BF16)
        pairs = pairs + mm(gs, ab, 1, 1)
        ga_ref[:, cols] = mm(mixed, gs, 1, 0).astype(BF16)
    pairs = jnp.where(rows >= columns, pairs, 0.0).astype(BF16)
    gb_ref[...] = mm(pairs, c, 0, 0)
    gc_ref[...] = mm(pairs, b, 1, 0)

    @pl.when(t == spans - 1)
    def _():
        finish(rounds - 1)


def quadrants(high_ref, low_ref, pair):
    span, size = high_ref.shape[0], pair.shape[0] // 2
    stacked = jnp.concatenate([high_ref[...], low_ref[...]], axis=0)
    products = mm(stacked, pair, 1, 1)
    rows = products[:span] + products[span:]
    return rows[:, :size] + rows[:, size:]


def shared_kernel(
    g_ref, dg_ref, act_ref, da_ref, lr_ref, prior_ref, before_ref, fresh_ref,
    entering_ref, arriving_ref, inner_b_ref, inner_c_ref,
    pair_ref, both_ref, states, carry,
):
    t = pl.program_id(0)
    span, channels = g_ref.shape
    half = span // 2
    size = carry.shape[0]

    @pl.when(t == 0)
    def _():
        carry[...] = arriving_ref[...]

    for cols in chunks_of(channels):
        lr = lr_ref[0, 0:1, cols]
        sb = jnp.exp((half + 1.0) * lr) * (
            before_ref[0, :, cols] + prior_ref[0, 0:1, cols] * entering_ref[:, cols]
        )
        hi = sb.astype(BF16)
        states[0:size, cols] = hi
        states[size : 2 * size, cols] = (sb - hi.astype(F32)).astype(BF16)
        held = carry[:, cols]
        ga = jnp.exp((half - 1.0) * lr) * held
        hi = ga.astype(BF16)
        pair_ref[0, 0:size, cols] = hi
        pair_ref[0, size : 2 * size, cols] = (ga - hi.astype(F32)).astype(BF16)
        carry[:, cols] = jnp.exp(span * lr) * held + fresh_ref[0, :, cols]
    both_ref[:, 0:size] = inner_b_ref[...] + quadrants(act_ref, da_ref, pair_ref[0])
    both_ref[:, size:] = inner_c_ref[...] + quadrants(g_ref, dg_ref, states[...])


def input_kernel(
    b_ref, w_ref, lr_ref, pair_ref, ga_ref, slope_ref,
    gx_ref, first_ref, gp,
):
    t = pl.program_id(0)
    span, channels = ga_ref.shape

    @pl.when(t == 0)
    def _():
        gp[span : span + 8] = jnp.zeros((8, channels), F32)

    @pl.when(t > 0)
    def _():
        gp[span : span + 8] = gp[0:8]

    twice = jnp.concatenate([b_ref[...], b_ref[...]], axis=1)
    for cols in chunks_of(channels):
        grad_act = mm(twice, pair_ref[0, :, cols], 1, 0) + ga_ref[:, cols].astype(F32)
        slope = slope_ref[:, cols].astype(F32) + 0.5
        gp[0:span, cols] = grad_act * decays(-lr_ref[0, 0:1, cols], span) * slope
        out = w_ref[0:1, cols] * gp[3 : 3 + span, cols]
        for k in range(1, 4):
            out = out + w_ref[k : k + 1, cols] * gp[3 - k : 3 - k + span, cols]
        gx_ref[:, cols] = out
    first_ref[...] = gp[0:8]


def shifted(array, axis, by):
    length = lax.axis_size(axis)
    return lax.ppermute(
        array, axis, [(i, i + by) for i in range(length) if 0 <= i + by < length]
    )


def swapped(array, axis, flip):
    return lax.ppermute(array, axis, [(i, i ^ flip) for i in range(lax.axis_size(axis))])


def half_sums(both):
    rows = both.shape[0] // 2
    odd = (lax.axis_index("hg") % 2) == 1
    low, high = both[:rows], both[rows:]
    return jnp.where(odd, high, low) + swapped(jnp.where(odd, low, high), "hg", 1)


def pair_sums(mine):
    flip = 2
    while flip < lax.axis_size("hg"):
        sent = mine.astype(BF16)
        mine = sent.astype(F32) + swapped(sent, "hg", flip).astype(F32)
        flip *= 2
    return mine


def joined_halves(mine):
    odd = (lax.axis_index("hg") % 2) == 1
    other = swapped(mine, "hg", 1)
    return jnp.concatenate([jnp.where(odd, other, mine), jnp.where(odd, mine, other)], axis=0)


def body(conv_input, grad_output, inject, readout, conv_weight, decay_codes):
    tokens, channels = conv_input.shape
    heads, spans = decay_codes.shape
    span = tokens // spans
    head_dim = channels // heads
    states = inject.shape[1]
    weights = conv_weight.astype(F32)
    log_rates = jnp.log1p(-decay_codes.astype(F32) * 1e-06)
    halo = shifted(conv_input[tokens - HALO :], "seq", 1)
    wide = jnp.repeat(log_rates.T, head_dim, axis=1)
    prior = jnp.exp(span * (jnp.cumsum(wide, axis=0) - wide))[:, None]
    own_log = span * jnp.sum(wide, axis=0, keepdims=True)
    lr = wide[:, None]
    step = span // HALO
    params = pltpu.CompilerParams(
        vmem_limit_bytes=48 << 20, dimension_semantics=("arbitrary",)
    )
    on = lambda t: t
    back = lambda t: spans - 1 - t

    def tile(at, width):
        return pl.BlockSpec((span, width), lambda t: (at(t), 0))

    def block(at, rows, width):
        return pl.BlockSpec((1, rows, width), lambda t: (at(t), 0, 0))

    def fixed(rows):
        return pl.BlockSpec((rows, channels), lambda t: (0, 0))

    def like(shape, dtype):
        return jax.ShapeDtypeStruct(shape, dtype)

    def cost(products, moved):
        return pl.CostEstimate(
            flops=2 * products * tokens * channels, bytes_accessed=moved, transcendentals=0
        )

    size = tokens * channels
    wide_tokens = like((tokens, channels), BF16)
    act, da, dg, slope, before, fresh, own_state, own_grad = pl.pallas_call(
        fold_kernel,
        grid=(spans,),
        in_specs=[
            tile(on, channels),
            pl.BlockSpec((HALO, channels), lambda t: (jnp.maximum(t * step - 1, 0), 0)),
            fixed(HALO),
            tile(on, channels),
            tile(on, states),
            tile(on, states),
            fixed(4),
            block(on, 1, channels),
        ],
        out_specs=[tile(on, channels)] * 4
        + [block(on, states, channels)] * 2
        + [fixed(states)] * 2,
        out_shape=[wide_tokens] * 4
        + [like((spans, states, channels), F32)] * 2
        + [like((states, channels), F32)] * 2,
        scratch_shapes=[
            pltpu.VMEM((span + HALO, channels), F32),
            pltpu.VMEM((8, channels), F32),
        ],
        compiler_params=params,
        cost_estimate=cost(4 * states, 16 * size),
        name="fold",
    )(conv_input, conv_input, halo, grad_output, inject, readout, weights, lr)

    length = lax.axis_size("seq")
    rounds = (length - 1).bit_length()
    inner_act, inner_b, inner_c, entering, arriving = pl.pallas_call(
        functools.partial(inner_kernel, length, rounds, "seq"),
        grid=(spans,),
        in_specs=[tile(on, channels)] * 4
        + [tile(on, states)] * 2
        + [fixed(states)] * 2
        + [fixed(1)],
        out_specs=[tile(on, channels)] + [tile(on, states)] * 2 + [fixed(states)] * 2,
        out_shape=[wide_tokens]
        + [like((tokens, states), F32)] * 2
        + [like((states, channels), F32)] * 2,
        scratch_shapes=[
            pltpu.VMEM((2, rounds, states + HALO, channels), BF16),
            pltpu.VMEM((2, rounds, states + HALO, channels), BF16),
            pltpu.VMEM((2, states, channels), F32),
            pltpu.VMEM((2, 8, channels), F32),
            pltpu.SemaphoreType.DMA((2, rounds)),
            pltpu.SemaphoreType.DMA((2, rounds)),
        ],
        compiler_params=pltpu.CompilerParams(
            vmem_limit_bytes=48 << 20,
            dimension_semantics=("arbitrary",),
            collective_id=0,
            has_side_effects=True,
        ),
        cost_estimate=cost(2 * span + states, 10 * size),
        name="inner",
    )(grad_output, dg, act, da, inject, readout, own_state, own_grad, own_log)
    pairs, both = pl.pallas_call(
        shared_kernel,
        grid=(spans,),
        in_specs=[tile(back, channels)] * 4
        + [block(back, 1, channels)] * 2
        + [block(back, states, channels)] * 2
        + [fixed(states)] * 2
        + [tile(back, states)] * 2,
        out_specs=[block(back, 2 * states, channels), tile(back, 2 * states)],
        out_shape=[
            like((spans, 2 * states, channels), BF16),
            like((tokens, 2 * states), F32),
        ],
        scratch_shapes=[
            pltpu.VMEM((2 * states, channels), BF16),
            pltpu.VMEM((states, channels), F32),
        ],
        compiler_params=params,
        cost_estimate=cost(8 * states, 14 * size),
        name="shared",
    )(grad_output, dg, act, da, lr, prior, before, fresh, entering, arriving, inner_b, inner_c)

    mine, pairs = lax.optimization_barrier((half_sums(both), pairs))
    grad_input, first = pl.pallas_call(
        input_kernel,
        grid=(spans,),
        in_specs=[
            tile(back, states),
            fixed(4),
            block(back, 1, channels),
            block(back, 2 * states, channels),
            tile(back, channels),
            tile(back, channels),
        ],
        out_specs=[tile(back, channels), fixed(8)],
        out_shape=[like((tokens, channels), F32), like((8, channels), F32)],
        scratch_shapes=[pltpu.VMEM((span + 8, channels), F32)],
        compiler_params=params,
        cost_estimate=cost(2 * states, 10 * size),
        name="inputs",
    )(inject, weights, lr, pairs, inner_act, slope)
    mine, first = lax.optimization_barrier((pair_sums(mine), first))
    later = shifted(first, "seq", -1)
    edge = jnp.stack(
        [sum(weights[k] * later[r - k] for k in range(r + 1)) for r in range(3)], axis=0
    )
    last = grad_input[tokens - 8 :] + jnp.pad(edge, ((5, 0), (0, 0)))
    grad_input = lax.dynamic_update_slice(grad_input, last, (tokens - 8, 0))
    total = joined_halves(mine)
    return grad_input, total[:, :states], total[:, states:]


def solution(mesh):
    return jax.shard_map(
        body,
        mesh=mesh,
        in_specs=(
            P("seq", "hg"),
            P("seq", "hg"),
            P("seq", None),
            P("seq", None),
            P(None, "hg"),
            P("hg", "seq"),
        ),
        out_specs=(P("seq", "hg"), P("seq", None), P("seq", None)),
        check_vma=False,
    )
```

time: 164 us -> 115 us (0.70)
  blocking collectives: 21.8 us -> 0 us
  waiting for transfers between devices: 28.2 us -> 7.16 us
  starting transfers between devices: 26.5 us -> 7.84 us
  Pallas kernels: 73.4 us -> 90.4 us
  local copies, waits for them, and re-layouts: 5.84 us -> 3.19 us
    unnamed x1 -> x0, blocking collectives: 21.8 us -> none
    ppermute x8 -> x2, starting transfers between devices: 24.7 us -> 6.12 us  [shifted(): lax.ppermute(array, axis, [(i, i + by) for i in range(length) if 0 <= i +...]
    pallas_call x2 -> x4, Pallas kernels: 73.4 us -> 90.4 us  [the longest x1 42.7 us: body(): pl.pallas_call(functools.partial(inner_kernel, length, rounds, 'seq'), gr...]
    ppermute x3, waiting for transfers between devices: 15.1 us -> 2.65 us  [swapped(): lax.ppermute(array, axis, [(i, i ^ flip) for i in range(lax.axis_size(axi...]
    ppermute x8 -> x2, waiting for transfers between devices: 13.1 us -> 4.51 us  [shifted(): lax.ppermute(array, axis, [(i, i + by) for i in range(length) if 0 <= i +...]
    unnamed x11 -> x10, local copies, waits for them, and re-layouts: 3.41 us -> 2.1 us
  transfers between devices with their start and end apart: 11 -> 5, of which waited for: 6 -> 2; matrix products, arithmetic and copies ran while one was open for 4% -> 3% of each run, Pallas kernels for 0% -> 11%
where the time goes in v1:
time: 115 us; the launch traced here: 114 us
  Pallas kernels  90.4 us (79%)
  starting transfers between devices  7.84 us (7%)
  waiting for transfers between devices  7.16 us (6%)
  other arithmetic  4.96 us (4%)
  local copies, waits for them, and re-layouts  3.19 us (3%)
    pallas_call x1, Pallas kernels, body(): pl.pallas_call(functools.partial(inner_kernel, length, rounds, 'seq'), gr...  42.7 us
    pallas_call x1, Pallas kernels, body(): pl.pallas_call(fold_kernel, grid=(spans,), in_specs=[tile(on, channels),...  22.3 us
    pallas_call x1, Pallas kernels, body(): pl.pallas_call(shared_kernel, grid=(spans,), in_specs=[tile(back, channel...  12.9 us
    pallas_call x1, Pallas kernels, body(): pl.pallas_call(input_kernel, grid=(spans,), in_specs=[tile(back, states),...  12.5 us
    ppermute x2, starting transfers between devices, shifted(): lax.ppermute(array, axis, [(i, i + by) for i in range(length) if 0 <= i +...  6.12 us
    ppermute x2, waiting for transfers between devices, shifted(): lax.ppermute(array, axis, [(i, i + by) for i in range(length) if 0 <= i +...  4.51 us
    ppermute x3, waiting for transfers between devices, swapped(): lax.ppermute(array, axis, [(i, i ^ flip) for i in range(lax.axis_size(axi...  2.65 us
  transfers between devices with their start and end apart: 5, of which 2 were waited for; matrix products, arithmetic and copies ran while one was open for 3% of the time, Pallas kernels for 11%

profile of v1, /device:TPU:0, one launch (start us, length us, event | category | flops | bytes accessed | tf_op | source)
XLA Modules:
  0.0 114.3 jit_solution(8308959054662238624)
XLA Ops:
  0.6 0.8 slice.42
  1.4 4.8 %collective-permute-start = (bf16[16,1024]{1,0:T(8,128)(2,1)S(1)}, bf16[16,1024]{1,0:T(8,128)(2,1)S(1)}, u32[]{:S(2)}, u32[]{:S(2)}) collective-permute-start(bf16[16,1024]{1,0:T(8,128)(2,1)S(1)} %slice.42), channel_id=1, source_target_pairs={{0,4},{4,8},{8,12},{12,16},{16,20},{20,24},{24,28},{1,5},{5,9},{9,... | collective-permute-start | bytes 98312 | tf_op jit(solution)/shard_map/ppermute | solution.py:280
  6.2 0.7 fusion.7
  6.9 0.1 broadcast_in_dim.2
  7.0 0.1 broadcast_in_dim_reshape.3.lr_ref
  7.1 0.1 fusion.1.prior_ref
  7.2 0.7 convert_element_type.17.w_ref
  7.9 0.1 reduce_sum.12
  8.0 0.1 mul.57.log_ref
  8.1 0.0 collective-permute-done.halo_ref
  8.1 1.0 copy-done
  9.1 1.0 copy-done.3
  10.2 22.3 %fold.1 = (bf16[2048,1024]{1,0:T(8,128)(2,1)}, bf16[2048,1024]{1,0:T(8,128)(2,1)}, bf16[2048,1024]{1,0:T(8,128)(2,1)}, bf16[2048,1024]{1,0:T(8,128)(2,1)}, f32[8...) custom-call(bf16[2048,1024]{1,0:T(8,128)(2,1)} %prev_ref.1, ...), custom_call_target="tpu_custom_call" | custom-call | flops 2147483648 | bytes 33554432 | tf_op jit(solution)/shard_map/fold/pallas_call | solution.py:350
  32.5 0.0 copy-done.1
  32.5 0.0 copy-done.4
  32.5 42.7 %inner.1 = (bf16[2048,1024]{1,0:T(8,128)(2,1)}, f32[2048,128]{1,0:T(8,128)S(1)}, f32[2048,128]{1,0:T(8,128)S(1)}, f32[128,1024]{1,0:T(8,128)S(1)}, f32[128,1024]{1,0:T(8,128)S(1)}) custom-call(bf16[2048,1024]{1,0:T(8,128)(2,1)} %g_ref.5, bf16[2048,1024]{1,0:T(8,128)(2,1)} %get-tuple-element.24.dg_ref, bf16[2048,1024]{1,0:T(8,128)(2,1)} %get-tuple-element.25.act_ref, ...), custom_call_target="tpu_custom_call" | custom-call | flops 2684354560 | bytes 20971520 | tf_op jit(solution)/shard_map/inner/pallas_call | solution.py:380
  75.2 12.9 %shared.1 = (bf16[8,256,1024]{2,1,0:T(8,128)(2,1)}, f32[2048,256]{1,0:T(8,128)S(1)}) custom-call(bf16[2048,1024]{1,0:T(8,128)(2,1)} %g_ref.5, bf16[2048,1024]{1,0:T(8,128)(2,1)} %get-tuple-element.24.dg_ref, bf16[2048,1024]{1,0:T(8,128)(2,1)} %get-tuple-element.25.act_ref, bf16[2048,1024]{1,0:T(8,128)(2,1)} %get-tuple-element.26.da_ref, ...), custom_call_target="tpu_custom_call" | custom-call | flops 4294967296 | bytes 29360128 | tf_op jit(solution)/shard_map/shared/pallas_call | solution.py:408
  88.1 0.1 slice_select_fusion
  88.2 0.1 collective-permute-start.1
  88.3 2.6 %collective-permute-done.1 = f32[1024,256]{1,0:T(8,128)S(1)} collective-permute-done((f32[1024,256]{1,0:T(8,128)S(1)}, f32[1024,256]{1,0:T(8,128)S(1)}, u32[]{:S(2)}, u32[]{:S(2)}) %collective-permute-start.1) | collective-permute-done | bytes 1048608 | tf_op jit(solution)/shard_map/ppermute | solution.py:286
  90.9 0.2 select_add_fusion
  91.2 1.6 %collective-permute-start.2 = (bf16[1024,256]{1,0:T(8,128)(2,1)S(1)}, bf16[1024,256]{1,0:T(8,128)(2,1)S(1)}, u32[]{:S(2)}, u32[]{:S(2)}) collective-permute-start(bf16[1024,256]{1,0:T(8,128)(2,1)S(1)} %select_add_fusion), channel_id=1, source_target_pairs={{0,2},{1,3},{2,0},{3,1},{4,6},{5,7},{6,4},{7,5},{8,10},{9,11},{10,... | collective-permute-start | bytes 1572872 | tf_op jit(solution)/shard_map/ppermute | solution.py:286
  92.8 12.5 %inputs.1 = (f32[2048,1024]{1,0:T(8,128)}, f32[8,1024]{1,0:T(8,128)S(1)}) custom-call(bf16[2048,128]{1,0:T(8,128)(2,1)S(1)} %copy-done.1, f32[4,1024]{1,0:T(4,128)S(1)} %convert_element_type.17.w_ref, f32[8,1,1024]{2,1,0:T(1,128)S(1)} %broadcast_in_dim_reshape.3.lr_ref, bf16[8,256,1024]{2,1,0:T(8,128)(2,1)S(1)} %copy-done.2, ...), custom_call_target="tpu_custom_call" | custom-call | flops 1073741824 | bytes 20971520 | tf_op jit(solution)/shard_map/inputs/pallas_call | solution.py:431
  105.2 0.0 collective-permute-done.2
  105.2 0.1 convert_add_fusion
  105.4 0.1 collective-permute-start.4
  105.4 1.3 %collective-permute-start.3 = (f32[8,1024]{1,0:T(8,128)S(1)}, f32[8,1024]{1,0:T(8,128)S(1)}, u32[]{:S(2)}, u32[]{:S(2)}) collective-permute-start(f32[8,1024]{1,0:T(8,128)S(1)} %get-tuple-element.43), channel_id=1, source_target_pairs={{4,0},{8,4},{12,8},{16,12},{20,16},{24,20},{28,24},{5,1},{9,5},{13... | collective-permute-start | bytes 98312 | tf_op jit(solution)/shard_map/ppermute | solution.py:280
  106.7 4.5 %collective-permute-done.3 = f32[8,1024]{1,0:T(8,128)S(1)} collective-permute-done((f32[8,1024]{1,0:T(8,128)S(1)}, f32[8,1024]{1,0:T(8,128)S(1)}, u32[]{:S(2)}, u32[]{:S(2)}) %collective-permute-start.3) | collective-permute-done | bytes 32800 | tf_op jit(solution)/shard_map/ppermute | solution.py:280
  111.3 1.4 %fusion.4 = f32[2048,1024]{1,0:T(8,128)} fusion(f32[2048,1024]{1,0:T(8,128)} %get-tuple-element.40, f32[1,1024]{1,0:T(1,128)S(1)} %get-tuple-element.50, f32[1,1024]{1,0:T(1,128)S(1)} %get-tuple-element.51, f32[1,1024]{1,0:T(1,128)S(1)} %get-tuple-element.49), kind=kLoop, calls=%fused_computation.14 | loop fusion | flops 57344 | bytes 77824 | tf_op jit(solution)/shard_map/dynamic_update_slice | solution.py:455
  112.7 0.0 collective-permute-done.4
  112.7 0.1 broadcast_select_fusion
  112.8 1.5 %pad_maximum_fusion = (f32[2048,128]{1,0:T(8,128)}, f32[2048,128]{1,0:T(8,128)}) fusion(f32[1024,256]{1,0:T(8,128)S(1)} %get-tuple-element.47, f32[1024,256]{1,0:T(8,128)S(1)} %get-tuple-element.48), kind=kLoop, calls=%fused_computation.6 | loop fusion | flops 524288 | bytes 4194304 | tf_op jit(solution)/shard_map/concatenate | solution.py:308
  (8 shorter events, 0.0 us)
Async XLA Ops:
  1.4 6.7 %collective-permute-start = (bf16[16,1024]{1,0:T(8,128)(2,1)S(1)}, bf16[16,1024]{1,0:T(8,128)(2,1)S(1)}, u32[]{:S(2)}, u32[]{:S(2)}) collective-permute-start(bf16[16,1024]{1,0:T(8,128)(2,1)S(1)} %slice.42), channel_id=1, source_target_pairs={{0,4},{4,8},{8,12},{12,16},{16,20},{20,24},{24,28},{1,5},{5,9},{9,... | collective-permute-start | bytes 98312 | tf_op jit(solution)/shard_map/ppermute | solution.py:280
  8.1 1.0 copy-start
  9.1 1.0 copy-start.3
  10.2 22.3 %copy-start.1 = (bf16[2048,128]{1,0:T(8,128)(2,1)S(1)}, bf16[2048,128]{1,0:T(8,128)(2,1)}, u32[]{:S(2)}) copy-start(bf16[2048,128]{1,0:T(8,128)(2,1)} %b_ref.5) | copy-start | bytes 1572868
  10.2 22.3 %copy-start.4 = (bf16[2048,128]{1,0:T(8,128)(2,1)S(1)}, bf16[2048,128]{1,0:T(8,128)(2,1)}, u32[]{:S(2)}) copy-start(bf16[2048,128]{1,0:T(8,128)(2,1)} %c_ref.3) | copy-start | bytes 1572868
  88.1 4.7 %copy-start.2 = (bf16[8,256,1024]{2,1,0:T(8,128)(2,1)S(1)}, bf16[8,256,1024]{2,1,0:T(8,128)(2,1)}, u32[]{:S(2)}) copy-start(bf16[8,256,1024]{2,1,0:T(8,128)(2,1)} %get-tuple-element.37.pair_ref) | copy-start | bytes 12582916
  88.2 2.7 %collective-permute-start.1 = (f32[1024,256]{1,0:T(8,128)S(1)}, f32[1024,256]{1,0:T(8,128)S(1)}, u32[]{:S(2)}, u32[]{:S(2)}) collective-permute-start(f32[1024,256]{1,0:T(8,128)S(1)} %slice_select_fusion), channel_id=1, source_target_pairs={{0,1},{1,0},{2,3},{3,2},{4,5},{5,4},{6,7},{7,6},{8,9},{9,8},{10,11... | collective-permute-start | bytes 3145736 | tf_op jit(solution)/shard_map/ppermute | solution.py:286
  91.2 14.1 %collective-permute-start.2 = (bf16[1024,256]{1,0:T(8,128)(2,1)S(1)}, bf16[1024,256]{1,0:T(8,128)(2,1)S(1)}, u32[]{:S(2)}, u32[]{:S(2)}) collective-permute-start(bf16[1024,256]{1,0:T(8,128)(2,1)S(1)} %select_add_fusion), channel_id=1, source_target_pairs={{0,2},{1,3},{2,0},{3,1},{4,6},{5,7},{6,4},{7,5},{8,10},{9,11},{10,... | collective-permute-start | bytes 1572872 | tf_op jit(solution)/shard_map/ppermute | solution.py:286
  105.4 7.3 %collective-permute-start.4 = (f32[1024,256]{1,0:T(8,128)S(1)}, f32[1024,256]{1,0:T(8,128)S(1)}, u32[]{:S(2)}, u32[]{:S(2)}) collective-permute-start(f32[1024,256]{1,0:T(8,128)S(1)} %convert_add_fusion), channel_id=1, source_target_pairs={{0,1},{1,0},{2,3},{3,2},{4,5},{5,4},{6,7},{7,6},{8,9},{9,8},{10,11... | collective-permute-start | bytes 3145736 | tf_op jit(solution)/shard_map/ppermute | solution.py:286
  105.4 5.8 %collective-permute-start.3 = (f32[8,1024]{1,0:T(8,128)S(1)}, f32[8,1024]{1,0:T(8,128)S(1)}, u32[]{:S(2)}, u32[]{:S(2)}) collective-permute-start(f32[8,1024]{1,0:T(8,128)S(1)} %get-tuple-element.43), channel_id=1, source_target_pairs={{4,0},{8,4},{12,8},{16,12},{20,16},{24,20},{28,24},{5,1},{9,5},{13... | collective-permute-start | bytes 98312 | tf_op jit(solution)/shard_map/ppermute | solution.py:280

commit v2 on v1

v2 whole, which is shorter than its diff:
```python
import functools

import jax
import jax.numpy as jnp
from jax import lax
from jax.experimental import pallas as pl
from jax.experimental.pallas import tpu as pltpu
from jax.sharding import PartitionSpec as P

F32 = jnp.float32
BF16 = jnp.bfloat16
HALO = 16


def mm(a, b, ca, cb):
    return lax.dot_general(a, b, (((ca,), (cb,)), ((), ())), preferred_element_type=F32)


WIDTH = 256


def chunks_of(channels):
    return [slice(i, i + WIDTH) for i in range(0, channels, WIDTH)]


def preact_of(xs, w_ref, at, span):
    v = w_ref[0:1] * xs[at + HALO - 3 : at + HALO - 3 + span]
    for k in range(1, 4):
        v = v + w_ref[k : k + 1] * xs[at + HALO - 3 + k : at + HALO - 3 + k + span]
    return v


def decays(lr, span):
    width = lr.shape[1]
    rows = lax.broadcasted_iota(jnp.int32, (8, width), 0)
    held = jnp.exp((rows - span // 2).astype(F32) * lr)
    length = 8
    while length < span:
        held = jnp.concatenate([held, held * jnp.exp(length * lr)], axis=0)
        length *= 2
    return held


def log_rows(log):
    high = log.astype(BF16).astype(F32)
    mid = (log - high).astype(BF16).astype(F32)
    low = log - high - mid
    rows = lax.broadcasted_iota(jnp.int32, (HALO, log.shape[1]), 0)
    tile = jnp.where(rows == 0, high, jnp.where(rows == 1, mid, jnp.where(rows == 2, low, 0.0)))
    return tile.astype(BF16)


def fold_kernel(
    length, rounds, axis, span,
    x_ref, prev_ref, halo_ref, g_ref, b_ref, c_ref, w_ref, lr_ref, log_ref,
    act_ref, da_ref, dg_ref, slope_ref, before_ref, fresh_ref,
    ga_ref, gb_ref, gc_ref, entering_ref, arriving_ref,
    xs, gs, ab, running, held, logs, sent, landed, send_sem, recv_sem,
):
    t = pl.program_id(0)
    chunks, size = held.shape[1], held.shape[2]
    rows, width = x_ref.shape
    parts = b_ref.shape[0] // rows
    spans = b_ref.shape[0] // span
    folding = chunks * parts
    half = span // 2
    me = lax.axis_index(axis)
    founds = (entering_ref, arriving_ref)

    def inside(device):
        return jnp.logical_and(device >= 0, device < length)

    def copy(way, n, r):
        by = (1 << r) * (1 - 2 * way)
        move = pltpu.make_async_remote_copy(
            src_ref=sent.at[way, n, r],
            dst_ref=landed.at[way, n, r],
            send_sem=send_sem.at[way, n, r],
            recv_sem=recv_sem.at[way, n, r],
            device_id={axis: me + by},
            device_id_type=pl.DeviceIdType.MESH,
        )
        return move, inside(me + by), inside(me - by)

    def start(n, r):
        for way in range(2):
            sent[way, n, r, 0:size] = held[way, n].astype(BF16)
            sent[way, n, r, size : size + HALO] = log_rows(logs[way, n, 0:1])
            move, sends, _ = copy(way, n, r)

            @pl.when(sends)
            def _():
                move.start()

    def finish(n, r):
        for way in range(2):
            move, sends, takes = copy(way, n, r)

            @pl.when(takes)
            def _():
                move.wait_recv()
                got = landed[way, n, r, 0:size].astype(F32)
                tail = landed[way, n, r, size : size + HALO].astype(F32)
                got_log = (tail[0:1] + tail[1:2]) + tail[2:3]
                found = founds[way]
                found[n] = found[n] + jnp.exp(logs[way, n, 1:2]) * got
                if r < rounds - 1:
                    held[way, n] = held[way, n] + jnp.exp(logs[way, n, 0:1]) * got
                    logs[way, n, 0:1] = logs[way, n, 0:1] + got_log
                    logs[way, n, 1:2] = logs[way, n, 1:2] + got_log

            @pl.when(sends)
            def _():
                move.wait_send()

    @pl.when(t == 0)
    def _():
        barrier = pltpu.get_barrier_semaphore()
        others = [me + sign * (1 << r) for r in range(rounds) for sign in (1, -1)]
        for other in others:

            @pl.when(inside(other))
            def _():
                pl.semaphore_signal(
                    barrier, inc=1, device_id={axis: other}, device_id_type=pl.DeviceIdType.MESH
                )

        pl.semaphore_wait(barrier, sum(jnp.where(inside(other), 1, 0) for other in others))
        held[...] = jnp.zeros_like(held)
        for way, found in enumerate(founds):
            found[...] = jnp.zeros_like(found)
            for n in range(chunks):
                logs[way, n, 0:1] = log_ref[n]
                logs[way, n, 1:2] = jnp.zeros((1, width), F32)

    @pl.when(t < folding)
    def _():
        n, part = t // parts, t % parts

        @pl.when(part == 0)
        def _():
            xs[0:HALO] = halo_ref[...].astype(F32)
            running[...] = jnp.zeros_like(running)

        @pl.when(part > 0)
        def _():
            xs[0:HALO] = prev_ref[...].astype(F32)

        xs[HALO : HALO + rows] = x_ref[...].astype(F32)
        for q in range(rows // span):
            at = q * span
            here = slice(at, at + span)
            place = pl.multiple_of(part * rows + at, span)
            lr = lr_ref[pl.ds(part * (rows // span) + q, 1)]
            b = b_ref[pl.ds(place, span)].T
            c = c_ref[pl.ds(place, span)].T
            v = preact_of(xs, w_ref, at, span)
            squashed = 0.5 + 0.5 * jnp.tanh(0.5 * v)
            full = v * squashed
            slope_ref[here] = (squashed + full * (1.0 - squashed) - 0.5).astype(BF16)
            a = full.astype(BF16)
            act_ref[here] = a
            af = a.astype(F32)
            more = af * (decays(-lr, span) - 1.0)
            da = more.astype(BF16)
            da_ref[here] = da
            ab[n, pl.ds(place, span)] = (af + more).astype(BF16)
            g = g_ref[here]
            gf = g.astype(F32)
            more = gf * (decays(lr, span) - 1.0)
            dg = more.astype(BF16)
            dg_ref[here] = dg
            gs[n, pl.ds(place, span)] = (gf + more).astype(BF16)
            fresh_state = jnp.exp((half - 1.0) * lr) * (mm(b, a, 1, 0) + mm(b, da, 1, 0))
            fresh_grad = jnp.exp((half + 1.0) * lr) * (mm(c, g, 1, 0) + mm(c, dg, 1, 0))
            state = held[0, n]
            before_ref[q] = state
            fresh_ref[q] = fresh_grad
            held[0, n] = jnp.exp(span * lr) * state + fresh_state
            held[1, n] = held[1, n] + jnp.exp(running[0:1]) * fresh_grad
            running[...] = running[...] + span * lr

    @pl.when(t >= folding)
    def _():
        place = pl.multiple_of((t - folding) * span, span)
        b, c = b_ref[pl.ds(place, span)], c_ref[pl.ds(place, span)]
        down = lax.broadcasted_iota(jnp.int32, (span, span), 0)
        along = lax.broadcasted_iota(jnp.int32, (span, span), 1)
        mixed = jnp.where(down <= along, mm(b, c, 1, 1), 0.0).astype(BF16)
        pairs = jnp.zeros((span, span), F32)
        for n in range(chunks):
            scaled = gs[n, pl.ds(place, span)]
            pairs = pairs + mm(scaled, ab[n, pl.ds(place, span)], 1, 1)
            ga_ref[:, n * width : (n + 1) * width] = mm(mixed, scaled, 1, 0).astype(BF16)
        pairs = jnp.where(down >= along, pairs, 0.0).astype(BF16)
        gb_ref[...] = mm(pairs, c, 0, 0)
        gc_ref[...] = mm(pairs, b, 1, 0)

    def step_of(n, r):
        step = parts * (n + 1) - 1 + 2 * r
        over = step - (folding - 1)
        return step if over <= 0 else folding - 1 + over * spans // (2 * rounds)

    for n in range(chunks):
        for r in range(rounds + 1):

            @pl.when(t == step_of(n, r))
            def _():
                if r > 0:
                    finish(n, r - 1)
                if r < rounds:
                    start(n, r)


def quadrants(high_ref, low_ref, pair):
    span, size = high_ref.shape[0], pair.shape[0] // 2
    stacked = jnp.concatenate([high_ref[...], low_ref[...]], axis=0)
    products = mm(stacked, pair, 1, 1)
    rows = products[:span] + products[span:]
    return rows[:, :size] + rows[:, size:]


def shared_kernel(
    g_ref, dg_ref, act_ref, da_ref, lr_ref, prior_ref, before_ref, fresh_ref,
    entering_ref, arriving_ref, inner_b_ref, inner_c_ref,
    pair_ref, both_ref, states, carry,
):
    t = pl.program_id(0)
    span, channels = g_ref.shape
    half = span // 2
    size = carry.shape[0]

    @pl.when(t == 0)
    def _():
        for n, cols in enumerate(chunks_of(channels)):
            carry[:, cols] = arriving_ref[n]

    for n, cols in enumerate(chunks_of(channels)):
        lr = lr_ref[0, 0:1, cols]
        sb = jnp.exp((half + 1.0) * lr) * (
            before_ref[0, :, cols] + prior_ref[0, 0:1, cols] * entering_ref[n]
        )
        hi = sb.astype(BF16)
        states[0:size, cols] = hi
        states[size : 2 * size, cols] = (sb - hi.astype(F32)).astype(BF16)
        held = carry[:, cols]
        ga = jnp.exp((half - 1.0) * lr) * held
        hi = ga.astype(BF16)
        pair_ref[0, 0:size, cols] = hi
        pair_ref[0, size : 2 * size, cols] = (ga - hi.astype(F32)).astype(BF16)
        carry[:, cols] = jnp.exp(span * lr) * held + fresh_ref[0, :, cols]
    both_ref[:, 0:size] = inner_b_ref[...] + quadrants(act_ref, da_ref, pair_ref[0])
    both_ref[:, size:] = inner_c_ref[...] + quadrants(g_ref, dg_ref, states[...])


def input_kernel(
    b_ref, w_ref, lr_ref, pair_ref, ga_ref, slope_ref,
    gx_ref, first_ref, gp,
):
    t = pl.program_id(0)
    span, channels = ga_ref.shape

    @pl.when(t == 0)
    def _():
        gp[span : span + 8] = jnp.zeros((8, channels), F32)

    @pl.when(t > 0)
    def _():
        gp[span : span + 8] = gp[0:8]

    twice = jnp.concatenate([b_ref[...], b_ref[...]], axis=1)
    for cols in chunks_of(channels):
        grad_act = mm(twice, pair_ref[0, :, cols], 1, 0) + ga_ref[:, cols].astype(F32)
        slope = slope_ref[:, cols].astype(F32) + 0.5
        gp[0:span, cols] = grad_act * decays(-lr_ref[0, 0:1, cols], span) * slope
        out = w_ref[0:1, cols] * gp[3 : 3 + span, cols]
        for k in range(1, 4):
            out = out + w_ref[k : k + 1, cols] * gp[3 - k : 3 - k + span, cols]
        gx_ref[:, cols] = out
    first_ref[...] = gp[0:8]


def shifted(array, axis, by):
    length = lax.axis_size(axis)
    return lax.ppermute(
        array, axis, [(i, i + by) for i in range(length) if 0 <= i + by < length]
    )


def swapped(array, axis, flip):
    return lax.ppermute(array, axis, [(i, i ^ flip) for i in range(lax.axis_size(axis))])


def half_sums(both):
    rows = both.shape[0] // 2
    odd = (lax.axis_index("hg") % 2) == 1
    low, high = both[:rows], both[rows:]
    return jnp.where(odd, high, low) + swapped(jnp.where(odd, low, high), "hg", 1)


def pair_sums(mine):
    flip = 2
    while flip < lax.axis_size("hg"):
        sent = mine.astype(BF16)
        mine = sent.astype(F32) + swapped(sent, "hg", flip).astype(F32)
        flip *= 2
    return mine


def joined_halves(mine):
    odd = (lax.axis_index("hg") % 2) == 1
    other = swapped(mine, "hg", 1)
    return jnp.concatenate([jnp.where(odd, other, mine), jnp.where(odd, mine, other)], axis=0)


def body(conv_input, grad_output, inject, readout, conv_weight, decay_codes):
    tokens, channels = conv_input.shape
    heads, spans = decay_codes.shape
    span = tokens // spans
    head_dim = channels // heads
    states = inject.shape[1]
    weights = conv_weight.astype(F32)
    log_rates = jnp.log1p(-decay_codes.astype(F32) * 1e-06)
    halo = shifted(conv_input[tokens - HALO :], "seq", 1)
    wide = jnp.repeat(log_rates.T, head_dim, axis=1)
    prior = jnp.exp(span * (jnp.cumsum(wide, axis=0) - wide))[:, None]
    own_log = span * jnp.sum(wide, axis=0, keepdims=True)
    lr = wide[:, None]
    params = pltpu.CompilerParams(
        vmem_limit_bytes=48 << 20, dimension_semantics=("arbitrary",)
    )
    on = lambda t: t
    back = lambda t: spans - 1 - t

    def tile(at, width):
        return pl.BlockSpec((span, width), lambda t: (at(t), 0))

    def block(at, rows, width):
        return pl.BlockSpec((1, rows, width), lambda t: (at(t), 0, 0))

    def fixed(rows):
        return pl.BlockSpec((rows, channels), lambda t: (0, 0))

    def like(shape, dtype):
        return jax.ShapeDtypeStruct(shape, dtype)

    def cost(products, moved):
        return pl.CostEstimate(
            flops=2 * products * tokens * channels, bytes_accessed=moved, transcendentals=0
        )

    size = tokens * channels
    wide_tokens = like((tokens, channels), BF16)
    length = lax.axis_size("seq")
    rounds = (length - 1).bit_length()
    chunks, parts = channels // WIDTH, 2
    rows = tokens // parts
    folding = chunks * parts

    def part_of(t):
        return jnp.minimum(t, folding - 1) % parts

    def chunk_of(t):
        return jnp.minimum(t, folding - 1) // parts

    def piece(height):
        return pl.BlockSpec((height, WIDTH), lambda t: (part_of(t), chunk_of(t)))

    def column(height):
        return pl.BlockSpec((height, WIDTH), lambda t: (0, chunk_of(t)))

    def whole(*shape):
        return pl.BlockSpec(shape, lambda t: (0,) * len(shape))

    late = lambda t: jnp.maximum(t - folding, 0)
    summary = pl.BlockSpec(
        (spans // parts, states, WIDTH), lambda t: (part_of(t), 0, chunk_of(t))
    )
    slots = pltpu.VMEM((2, chunks, rounds, states + HALO, WIDTH), BF16)
    scaled = pltpu.VMEM((chunks, tokens, WIDTH), BF16)
    (
        act, da, dg, slope, before, fresh, inner_act, inner_b, inner_c, entering, arriving
    ) = pl.pallas_call(
        functools.partial(fold_kernel, length, rounds, "seq", span),
        grid=(folding + spans,),
        in_specs=[
            piece(rows),
            pl.BlockSpec(
                (HALO, WIDTH),
                lambda t: (jnp.maximum(part_of(t) * (rows // HALO) - 1, 0), chunk_of(t)),
            ),
            column(HALO),
            piece(rows),
            whole(tokens, states),
            whole(tokens, states),
            column(4),
            column(spans),
            whole(chunks, 1, WIDTH),
        ],
        out_specs=[piece(rows)] * 4
        + [summary] * 2
        + [tile(late, channels)]
        + [tile(late, states)] * 2
        + [whole(chunks, states, WIDTH)] * 2,
        out_shape=[wide_tokens] * 4
        + [like((spans, states, channels), F32)] * 2
        + [wide_tokens]
        + [like((tokens, states), F32)] * 2
        + [like((chunks, states, WIDTH), F32)] * 2,
        scratch_shapes=[
            pltpu.VMEM((rows + HALO, WIDTH), F32),
            scaled,
            scaled,
            pltpu.VMEM((8, WIDTH), F32),
            pltpu.VMEM((2, chunks, states, WIDTH), F32),
            pltpu.VMEM((2, chunks, 8, WIDTH), F32),
            slots,
            slots,
            pltpu.SemaphoreType.DMA((2, chunks, rounds)),
            pltpu.SemaphoreType.DMA((2, chunks, rounds)),
        ],
        compiler_params=pltpu.CompilerParams(
            vmem_limit_bytes=56 << 20,
            dimension_semantics=("arbitrary",),
            collective_id=0,
            has_side_effects=True,
        ),
        cost_estimate=cost(2 * span + 5 * states, 20 * size),
        name="fold",
    )(
        conv_input, conv_input, halo, grad_output, inject, readout, weights, wide,
        own_log.reshape(chunks, 1, WIDTH),
    )
    pairs, both = pl.pallas_call(
        shared_kernel,
        grid=(spans,),
        in_specs=[tile(back, channels)] * 4
        + [block(back, 1, channels)] * 2
        + [block(back, states, channels)] * 2
        + [whole(chunks, states, WIDTH)] * 2
        + [tile(back, states)] * 2,
        out_specs=[block(back, 2 * states, channels), tile(back, 2 * states)],
        out_shape=[
            like((spans, 2 * states, channels), BF16),
            like((tokens, 2 * states), F32),
        ],
        scratch_shapes=[
            pltpu.VMEM((2 * states, channels), BF16),
            pltpu.VMEM((states, channels), F32),
        ],
        compiler_params=params,
        cost_estimate=cost(8 * states, 14 * size),
        name="shared",
    )(grad_output, dg, act, da, lr, prior, before, fresh, entering, arriving, inner_b, inner_c)

    mine, pairs = lax.optimization_barrier((half_sums(both), pairs))
    grad_input, first = pl.pallas_call(
        input_kernel,
        grid=(spans,),
        in_specs=[
            tile(back, states),
            fixed(4),
            block(back, 1, channels),
            block(back, 2 * states, channels),
            tile(back, channels),
            tile(back, channels),
        ],
        out_specs=[tile(back, channels), fixed(8)],
        out_shape=[like((tokens, channels), F32), like((8, channels), F32)],
        scratch_shapes=[pltpu.VMEM((span + 8, channels), F32)],
        compiler_params=params,
        cost_estimate=cost(2 * states, 10 * size),
        name="inputs",
    )(inject, weights, lr, pairs, inner_act, slope)
    mine, first = lax.optimization_barrier((pair_sums(mine), first))
    later = shifted(first, "seq", -1)
    edge = jnp.stack(
        [sum(weights[k] * later[r - k] for k in range(r + 1)) for r in range(3)], axis=0
    )
    last = grad_input[tokens - 8 :] + jnp.pad(edge, ((5, 0), (0, 0)))
    grad_input = lax.dynamic_update_slice(grad_input, last, (tokens - 8, 0))
    total = joined_halves(mine)
    return grad_input, total[:, :states], total[:, states:]


def solution(mesh):
    return jax.shard_map(
        body,
        mesh=mesh,
        in_specs=(
            P("seq", "hg"),
            P("seq", "hg"),
            P("seq", None),
            P("seq", None),
            P(None, "hg"),
            P("hg", "seq"),
        ),
        out_specs=(P("seq", "hg"), P("seq", None), P("seq", None)),
        check_vma=False,
    )
```

time: 115 us -> 104 us (0.904)
  Pallas kernels: 90.4 us -> 73 us
  local copies, waits for them, and re-layouts: 3.19 us -> 7.63 us
    pallas_call x2 -> x1, Pallas kernels: 65 us -> 47.7 us  [body(): pl.pallas_call(functools.partial(fold_kernel, length, rounds, 'seq', span...]
    unnamed x10 -> x16, local copies, waits for them, and re-layouts: 2.1 us -> 5.15 us
  transfers between devices with their start and end apart: 5 -> 5, of which waited for: 2 -> 2; matrix products, arithmetic and copies ran while one was open for 3% -> 5% of each run, Pallas kernels for 11% -> 12%
where the time goes in v2:
time: 104 us; the launch traced here: 103 us
  Pallas kernels  73 us (70%)
  starting transfers between devices  8.64 us (8%)
  waiting for transfers between devices  7.85 us (8%)
  local copies, waits for them, and re-layouts  7.63 us (7%)
  other arithmetic  5.57 us (5%)
    pallas_call x1, Pallas kernels, body(): pl.pallas_call(functools.partial(fold_kernel, length, rounds, 'seq', span...  47.7 us
    pallas_call x1, Pallas kernels, body(): pl.pallas_call(shared_kernel, grid=(spans,), in_specs=[tile(back, channel...  12.8 us
    pallas_call x1, Pallas kernels, body(): pl.pallas_call(input_kernel, grid=(spans,), in_specs=[tile(back, states),...  12.5 us
    ppermute x2, starting transfers between devices, shifted(): lax.ppermute(array, axis, [(i, i + by) for i in range(length) if 0 <= i +...  6.12 us
    ppermute x2, waiting for transfers between devices, shifted(): lax.ppermute(array, axis, [(i, i + by) for i in range(length) if 0 <= i +...  5.2 us
    unnamed x16, local copies, waits for them, and re-layouts  5.15 us
    ppermute x3, waiting for transfers between devices, swapped(): lax.ppermute(array, axis, [(i, i ^ flip) for i in range(lax.axis_size(axi...  2.65 us
    ppermute x3, starting transfers between devices, swapped(): lax.ppermute(array, axis, [(i, i ^ flip) for i in range(lax.axis_size(axi...  2.52 us
  transfers between devices with their start and end apart: 5, of which 2 were waited for; matrix products, arithmetic and copies ran while one was open for 5% of the time, Pallas kernels for 12%

profile of v2, /device:TPU:0, one launch (start us, length us, event | category | flops | bytes accessed | tf_op | source)
XLA Modules:
  0.0 103.5 jit_solution(13281879520884729362)
XLA Ops:
  0.6 0.8 slice.42
  1.4 4.8 %collective-permute-start = (bf16[16,1024]{1,0:T(8,128)(2,1)S(1)}, bf16[16,1024]{1,0:T(8,128)(2,1)S(1)}, u32[]{:S(2)}, u32[]{:S(2)}) collective-permute-start(bf16[16,1024]{1,0:T(8,128)(2,1)S(1)} %slice.42), channel_id=1, source_target_pairs={{0,4},{4,8},{8,12},{12,16},{16,20},{20,24},{24,28},{1,5},{5,9},{9,... | collective-permute-start | bytes 98312 | tf_op jit(solution)/shard_map/ppermute | solution.py:285
  6.2 0.7 fusion.7
  6.9 0.1 broadcast_in_dim.2
  7.0 0.1 broadcast_in_dim_reshape.3.lr_ref
  7.1 0.1 fusion.1.prior_ref
  7.2 0.7 reshape.57.lr_ref
  7.9 1.3 %convert_element_type.17.w_ref = f32[4,1024]{1,0:T(4,128)} convert(bf16[4,1024]{1,0:T(4,128)(2,1)} %param.10) | non-fusion elementwise | flops 4096 | bytes 24576 | tf_op jit(solution)/shard_map/convert_element_type | solution.py:322
  9.2 0.1 mul.69
  9.3 0.1 reduce_sum.12
  9.4 0.7 mul.70.log_ref
  10.0 0.0 collective-permute-done.halo_ref
  10.0 0.6 copy-done.7
  10.7 47.7 %fold.1 = (bf16[2048,1024]{1,0:T(8,128)(2,1)}, bf16[2048,1024]{1,0:T(8,128)(2,1)}, bf16[2048,1024]{1,0:T(8,128)(2,1)}, bf16[2048,1024]{1,0:T(8,128)(2,1)}, f32[8...) custom-call(bf16[2048,1024]{1,0:T(8,128)(2,1)} %prev_ref.1, ...), custom_call_target="tpu_custom_call" | custom-call | flops 4831838208 | bytes 41943040 | tf_op jit(solution)/shard_map/fold/pallas_call | solution.py:383
  58.4 1.2 %copy-done.1 = f32[2048,128]{1,0:T(8,128)S(1)} copy-done((f32[2048,128]{1,0:T(8,128)S(1)}, f32[2048,128]{1,0:T(8,128)}, u32[]{:S(2)}) %copy-start.1) | copy-done | bytes 1048600
  59.6 1.2 %copy-done.2 = f32[2048,128]{1,0:T(8,128)S(1)} copy-done((f32[2048,128]{1,0:T(8,128)S(1)}, f32[2048,128]{1,0:T(8,128)}, u32[]{:S(2)}) %copy-start.2) | copy-done | bytes 1048600
  60.9 1.0 %copy-done.3 = f32[4,128,256]{2,1,0:T(8,128)S(1)} copy-done((f32[4,128,256]{2,1,0:T(8,128)S(1)}, f32[4,128,256]{2,1,0:T(8,128)}, u32[]{:S(2)}) %copy-start.3) | copy-done | bytes 524312
  61.9 1.0 %copy-done.4 = f32[4,128,256]{2,1,0:T(8,128)S(1)} copy-done((f32[4,128,256]{2,1,0:T(8,128)S(1)}, f32[4,128,256]{2,1,0:T(8,128)}, u32[]{:S(2)}) %copy-start.4) | copy-done | bytes 524312
  62.9 12.8 %shared.1 = (bf16[8,256,1024]{2,1,0:T(8,128)(2,1)}, f32[2048,256]{1,0:T(8,128)S(1)}) custom-call(bf16[2048,1024]{1,0:T(8,128)(2,1)} %g_ref.3, bf16[2048,1024]{1,0:T(8,128)(2,1)} %get-tuple-element.22.dg_ref, bf16[2048,1024]{1,0:T(8,128)(2,1)} %get-tuple-element.23.act_ref, bf16[2048,1024]{1,0:T(8,128)(2,1)} %get-tuple-element.24.da_ref, ...), custom_call_target="tpu_custom_call" | custom-call | flops 4294967296 | bytes 29360128 | tf_op jit(solution)/shard_map/shared/pallas_call | solution.py:434
  75.8 0.1 slice_select_fusion
  75.9 0.1 collective-permute-start.1
  76.0 2.6 %collective-permute-done.1 = f32[1024,256]{1,0:T(8,128)S(1)} collective-permute-done((f32[1024,256]{1,0:T(8,128)S(1)}, f32[1024,256]{1,0:T(8,128)S(1)}, u32[]{:S(2)}, u32[]{:S(2)}) %collective-permute-start.1) | collective-permute-done | bytes 1048608 | tf_op jit(solution)/shard_map/ppermute | solution.py:291
  78.6 0.3 select_add_fusion
  78.9 2.4 %collective-permute-start.2 = (bf16[1024,256]{1,0:T(8,128)(2,1)S(1)}, bf16[1024,256]{1,0:T(8,128)(2,1)S(1)}, u32[]{:S(2)}, u32[]{:S(2)}) collective-permute-start(bf16[1024,256]{1,0:T(8,128)(2,1)S(1)} %select_add_fusion), channel_id=1, source_target_pairs={{0,2},{1,3},{2,0},{3,1},{4,6},{5,7},{6,4},{7,5},{8,10},{9,11},{10,... | collective-permute-start | bytes 1572872 | tf_op jit(solution)/shard_map/ppermute | solution.py:291
  81.3 12.5 %inputs.1 = (f32[2048,1024]{1,0:T(8,128)}, f32[8,1024]{1,0:T(8,128)S(1)}) custom-call(bf16[2048,128]{1,0:T(8,128)(2,1)S(1)} %copy-done.5, f32[4,1024]{1,0:T(4,128)S(1)} %copy-done.6, f32[8,1,1024]{2,1,0:T(1,128)S(1)} %broadcast_in_dim_reshape.3.lr_ref, bf16[8,256,1024]{2,1,0:T(8,128)(2,1)S(1)} %copy-done, bf16[2048,1024]{1,0:T(8,128)(2,1)} %get-tuple-element.34.ga_ref, ...), custom_call_target="tpu_custom_call" | custom-call | flops 1073741824 | bytes 20971520 | tf_op jit(solution)/shard_map/inputs/pallas_call | solution.py:457
  93.8 0.1 convert_add_fusion
  93.9 0.1 collective-permute-start.4
  94.0 1.3 %collective-permute-start.3 = (f32[8,1024]{1,0:T(8,128)S(1)}, f32[8,1024]{1,0:T(8,128)S(1)}, u32[]{:S(2)}, u32[]{:S(2)}) collective-permute-start(f32[8,1024]{1,0:T(8,128)S(1)} %get-tuple-element.39), channel_id=1, source_target_pairs={{4,0},{8,4},{12,8},{16,12},{20,16},{24,20},{28,24},{5,1},{9,5},{13... | collective-permute-start | bytes 98312 | tf_op jit(solution)/shard_map/ppermute | solution.py:285
  95.3 5.2 %collective-permute-done.3 = f32[8,1024]{1,0:T(8,128)S(1)} collective-permute-done((f32[8,1024]{1,0:T(8,128)S(1)}, f32[8,1024]{1,0:T(8,128)S(1)}, u32[]{:S(2)}, u32[]{:S(2)}) %collective-permute-start.3) | collective-permute-done | bytes 32800 | tf_op jit(solution)/shard_map/ppermute | solution.py:285
  100.5 1.4 %fusion.4 = f32[2048,1024]{1,0:T(8,128)} fusion(f32[2048,1024]{1,0:T(8,128)} %get-tuple-element.36, f32[1,1024]{1,0:T(1,128)S(1)} %get-tuple-element.46, f32[1,1024]{1,0:T(1,128)S(1)} %get-tuple-element.47, f32[1,1024]{1,0:T(1,128)S(1)} %get-tuple-element.45), kind=kLoop, calls=%fused_computation.14 | loop fusion | flops 57344 | bytes 77824 | tf_op jit(solution)/shard_map/dynamic_update_slice | solution.py:481
  101.9 0.1 broadcast_select_fusion
  102.0 1.5 %pad_maximum_fusion = (f32[2048,128]{1,0:T(8,128)}, f32[2048,128]{1,0:T(8,128)}) fusion(f32[1024,256]{1,0:T(8,128)S(1)} %get-tuple-element.43, f32[1024,256]{1,0:T(8,128)S(1)} %get-tuple-element.44), kind=kLoop, calls=%fused_computation.6 | loop fusion | flops 524288 | bytes 4194304 | tf_op jit(solution)/shard_map/concatenate | solution.py:313
  (15 shorter events, 0.1 us)
Async XLA Ops:
  1.4 8.6 %collective-permute-start = (bf16[16,1024]{1,0:T(8,128)(2,1)S(1)}, bf16[16,1024]{1,0:T(8,128)(2,1)S(1)}, u32[]{:S(2)}, u32[]{:S(2)}) collective-permute-start(bf16[16,1024]{1,0:T(8,128)(2,1)S(1)} %slice.42), channel_id=1, source_target_pairs={{0,4},{4,8},{8,12},{12,16},{16,20},{20,24},{24,28},{1,5},{5,9},{9,... | collective-permute-start | bytes 98312 | tf_op jit(solution)/shard_map/ppermute | solution.py:285
  10.0 0.6 copy-start.7
  58.4 1.2 %copy-start.1 = (f32[2048,128]{1,0:T(8,128)S(1)}, f32[2048,128]{1,0:T(8,128)}, u32[]{:S(2)}) copy-start(f32[2048,128]{1,0:T(8,128)} %get-tuple-element.29.inner_b_ref) | copy-start | bytes 3145732
  59.6 1.2 %copy-start.2 = (f32[2048,128]{1,0:T(8,128)S(1)}, f32[2048,128]{1,0:T(8,128)}, u32[]{:S(2)}) copy-start(f32[2048,128]{1,0:T(8,128)} %get-tuple-element.30.inner_c_ref) | copy-start | bytes 3145732
  60.9 1.0 %copy-start.3 = (f32[4,128,256]{2,1,0:T(8,128)S(1)}, f32[4,128,256]{2,1,0:T(8,128)}, u32[]{:S(2)}) copy-start(f32[4,128,256]{2,1,0:T(8,128)} %get-tuple-element.27.entering_ref) | copy-start | bytes 1572868
  61.9 1.0 %copy-start.4 = (f32[4,128,256]{2,1,0:T(8,128)S(1)}, f32[4,128,256]{2,1,0:T(8,128)}, u32[]{:S(2)}) copy-start(f32[4,128,256]{2,1,0:T(8,128)} %get-tuple-element.28.arriving_ref) | copy-start | bytes 1572868
  75.7 5.5 %copy-start = (bf16[8,256,1024]{2,1,0:T(8,128)(2,1)S(1)}, bf16[8,256,1024]{2,1,0:T(8,128)(2,1)}, u32[]{:S(2)}) copy-start(bf16[8,256,1024]{2,1,0:T(8,128)(2,1)} %get-tuple-element.33.pair_ref) | copy-start | bytes 12582916
  75.7 5.5 %copy-start.5 = (bf16[2048,128]{1,0:T(8,128)(2,1)S(1)}, bf16[2048,128]{1,0:T(8,128)(2,1)}, u32[]{:S(2)}) copy-start(bf16[2048,128]{1,0:T(8,128)(2,1)} %b_ref.3) | copy-start | bytes 1572868
  75.8 5.5 %copy-start.6 = (f32[4,1024]{1,0:T(4,128)S(1)}, f32[4,1024]{1,0:T(4,128)}, u32[]{:S(2)}) copy-start(f32[4,1024]{1,0:T(4,128)} %convert_element_type.17.w_ref) | copy-start | bytes 49156
  75.9 2.7 %collective-permute-start.1 = (f32[1024,256]{1,0:T(8,128)S(1)}, f32[1024,256]{1,0:T(8,128)S(1)}, u32[]{:S(2)}, u32[]{:S(2)}) collective-permute-start(f32[1024,256]{1,0:T(8,128)S(1)} %slice_select_fusion), channel_id=1, source_target_pairs={{0,1},{1,0},{2,3},{3,2},{4,5},{5,4},{6,7},{7,6},{8,9},{9,8},{10,11... | collective-permute-start | bytes 3145736 | tf_op jit(solution)/shard_map/ppermute | solution.py:291
  78.9 14.9 %collective-permute-start.2 = (bf16[1024,256]{1,0:T(8,128)(2,1)S(1)}, bf16[1024,256]{1,0:T(8,128)(2,1)S(1)}, u32[]{:S(2)}, u32[]{:S(2)}) collective-permute-start(bf16[1024,256]{1,0:T(8,128)(2,1)S(1)} %select_add_fusion), channel_id=1, source_target_pairs={{0,2},{1,3},{2,0},{3,1},{4,6},{5,7},{6,4},{7,5},{8,10},{9,11},{10,... | collective-permute-start | bytes 1572872 | tf_op jit(solution)/shard_map/ppermute | solution.py:291
  93.9 8.0 %collective-permute-start.4 = (f32[1024,256]{1,0:T(8,128)S(1)}, f32[1024,256]{1,0:T(8,128)S(1)}, u32[]{:S(2)}, u32[]{:S(2)}) collective-permute-start(f32[1024,256]{1,0:T(8,128)S(1)} %convert_add_fusion), channel_id=1, source_target_pairs={{0,1},{1,0},{2,3},{3,2},{4,5},{5,4},{6,7},{7,6},{8,9},{9,8},{10,11... | collective-permute-start | bytes 3145736 | tf_op jit(solution)/shard_map/ppermute | solution.py:291
  94.0 6.5 %collective-permute-start.3 = (f32[8,1024]{1,0:T(8,128)S(1)}, f32[8,1024]{1,0:T(8,128)S(1)}, u32[]{:S(2)}, u32[]{:S(2)}) collective-permute-start(f32[8,1024]{1,0:T(8,128)S(1)} %get-tuple-element.39), channel_id=1, source_target_pairs={{4,0},{8,4},{12,8},{16,12},{20,16},{24,20},{28,24},{5,1},{9,5},{13... | collective-permute-start | bytes 98312 | tf_op jit(solution)/shard_map/ppermute | solution.py:285

commit v3 on v2

--- a/solution.py
+++ b/solution.py
@@ -52,10 +52,10 @@
 
 def fold_kernel(
     length, rounds, axis, span,
-    x_ref, prev_ref, halo_ref, g_ref, b_ref, c_ref, w_ref, lr_ref, log_ref,
+    x_ref, prev_ref, all_ref, g_ref, b_ref, c_ref, w_ref, lr_ref, log_ref,
     act_ref, da_ref, dg_ref, slope_ref, before_ref, fresh_ref,
     ga_ref, gb_ref, gc_ref, entering_ref, arriving_ref,
-    xs, gs, ab, running, held, logs, sent, landed, send_sem, recv_sem,
+    xs, gs, ab, running, held, logs, sent, landed, halo, send_sem, recv_sem, halo_sem,
 ):
     t = pl.program_id(0)
     chunks, size = held.shape[1], held.shape[2]
@@ -126,6 +126,19 @@
                 )
 
         pl.semaphore_wait(barrier, sum(jnp.where(inside(other), 1, 0) for other in others))
+        move = pltpu.make_async_remote_copy(
+            src_ref=all_ref.at[pl.ds(all_ref.shape[0] - HALO, HALO)],
+            dst_ref=halo,
+            send_sem=halo_sem.at[0],
+            recv_sem=halo_sem.at[1],
+            device_id={axis: me + 1},
+            device_id_type=pl.DeviceIdType.MESH,
+        )
+
+        @pl.when(inside(me + 1))
+        def _():
+            move.start()
+
         held[...] = jnp.zeros_like(held)
         for way, found in enumerate(founds):
             found[...] = jnp.zeros_like(found)
@@ -133,13 +146,25 @@
                 logs[way, n, 0:1] = log_ref[n]
                 logs[way, n, 1:2] = jnp.zeros((1, width), F32)
 
+        @pl.when(me == 0)
+        def _():
+            halo[...] = jnp.zeros_like(halo)
+
+        @pl.when(me > 0)
+        def _():
+            move.wait_recv()
+
+        @pl.when(inside(me + 1))
+        def _():
+            move.wait_send()
+
     @pl.when(t < folding)
     def _():
         n, part = t // parts, t % parts
 
         @pl.when(part == 0)
         def _():
-            xs[0:HALO] = halo_ref[...].astype(F32)
+            xs[0:HALO] = halo[:, pl.ds(pl.multiple_of(n * width, width), width)].astype(F32)
             running[...] = jnp.zeros_like(running)
 
         @pl.when(part > 0)
@@ -321,13 +346,12 @@
     states = inject.shape[1]
     weights = conv_weight.astype(F32)
     log_rates = jnp.log1p(-decay_codes.astype(F32) * 1e-06)
-    halo = shifted(conv_input[tokens - HALO :], "seq", 1)
     wide = jnp.repeat(log_rates.T, head_dim, axis=1)
     prior = jnp.exp(span * (jnp.cumsum(wide, axis=0) - wide))[:, None]
     own_log = span * jnp.sum(wide, axis=0, keepdims=True)
     lr = wide[:, None]
     params = pltpu.CompilerParams(
-        vmem_limit_bytes=48 << 20, dimension_semantics=("arbitrary",)
+        vmem_limit_bytes=60 << 20, dimension_semantics=("arbitrary",)
     )
     on = lambda t: t
     back = lambda t: spans - 1 - t
@@ -389,7 +413,7 @@
                 (HALO, WIDTH),
                 lambda t: (jnp.maximum(part_of(t) * (rows // HALO) - 1, 0), chunk_of(t)),
             ),
-            column(HALO),
+            pl.BlockSpec(memory_space=pl.ANY),
             piece(rows),
             whole(tokens, states),
             whole(tokens, states),
@@ -416,11 +440,13 @@
             pltpu.VMEM((2, chunks, 8, WIDTH), F32),
             slots,
             slots,
+            pltpu.VMEM((HALO, channels), BF16),
             pltpu.SemaphoreType.DMA((2, chunks, rounds)),
             pltpu.SemaphoreType.DMA((2, chunks, rounds)),
+            pltpu.SemaphoreType.DMA((2,)),
         ],
         compiler_params=pltpu.CompilerParams(
-            vmem_limit_bytes=56 << 20,
+            vmem_limit_bytes=60 << 20,
             dimension_semantics=("arbitrary",),
             collective_id=0,
             has_side_effects=True,
@@ -428,7 +454,7 @@
         cost_estimate=cost(2 * span + 5 * states, 20 * size),
         name="fold",
     )(
-        conv_input, conv_input, halo, grad_output, inject, readout, weights, wide,
+        conv_input, conv_input, conv_input, grad_output, inject, readout, weights, wide,
         own_log.reshape(chunks, 1, WIDTH),
     )
     pairs, both = pl.pallas_call(

time: 104 us -> 104 us (level)
  Pallas kernels: 73 us -> 81.8 us
  local copies, waits for them, and re-layouts: 7.63 us -> 1.74 us
  starting transfers between devices: 8.64 us -> 3.02 us
  other arithmetic: 5.57 us -> 7.87 us
    pallas_call x1, Pallas kernels: 47.7 us -> 53.3 us  [body(): pl.pallas_call(functools.partial(fold_kernel, length, rounds, 'seq', span...]
    unnamed x16 -> x6, local copies, waits for them, and re-layouts: 5.15 us -> 0.02 us
    ppermute x2 -> x1, starting transfers between devices: 6.12 us -> 1.29 us  [shifted(): lax.ppermute(array, axis, [(i, i + by) for i in range(length) if 0 <= i +...]
    pallas_call x1, Pallas kernels: 12.8 us -> 14.8 us  [body(): pl.pallas_call(shared_kernel, grid=(spans,), in_specs=[tile(back, channel...]
    select_n x1, other arithmetic: 0.14 us -> 1.82 us  [half_sums(): jnp.where(odd, low, high)]
    pallas_call x1, Pallas kernels: 12.5 us -> 13.8 us  [body(): pl.pallas_call(input_kernel, grid=(spans,), in_specs=[tile(back, states),...]
    ppermute x2 -> x1, waiting for transfers between devices: 5.2 us -> 5.27 us  [shifted(): lax.ppermute(array, axis, [(i, i + by) for i in range(length) if 0 <= i +...]
  transfers between devices with their start and end apart: 5 -> 4, of which waited for: 2 -> 2; matrix products, arithmetic and copies ran while one was open for 5% -> 1% of each run, Pallas kernels for 12% -> 13%
where the time goes in v3:
time: 104 us; the launch traced here: 103 us
  Pallas kernels  81.8 us (79%)
  waiting for transfers between devices  7.92 us (8%)
  other arithmetic  7.87 us (8%)
  starting transfers between devices  3.02 us (3%)
  local copies, waits for them, and re-layouts  1.74 us (2%)
    pallas_call x1, Pallas kernels, body(): pl.pallas_call(functools.partial(fold_kernel, length, rounds, 'seq', span...  53.3 us
    pallas_call x1, Pallas kernels, body(): pl.pallas_call(shared_kernel, grid=(spans,), in_specs=[tile(back, channel...  14.8 us
    pallas_call x1, Pallas kernels, body(): pl.pallas_call(input_kernel, grid=(spans,), in_specs=[tile(back, states),...  13.8 us
    ppermute x1, waiting for transfers between devices, shifted(): lax.ppermute(array, axis, [(i, i + by) for i in range(length) if 0 <= i +...  5.27 us
    ppermute x3, waiting for transfers between devices, swapped(): lax.ppermute(array, axis, [(i, i ^ flip) for i in range(lax.axis_size(axi...  2.65 us
  transfers between devices with their start and end apart: 4, of which 2 were waited for; matrix products, arithmetic and copies ran while one was open for 1% of the time, Pallas kernels for 13%

profile of v3, /device:TPU:0, one launch (start us, length us, event | category | flops | bytes accessed | tf_op | source)
XLA Modules:
  0.0 103.1 jit_solution(17784086415074924009)
XLA Ops:
  0.6 0.7 fusion.7
  1.3 0.1 broadcast_in_dim.2
  1.4 0.7 reshape.57.lr_ref
  2.1 0.1 broadcast_in_dim_reshape.3.lr_ref
  2.2 0.0 copy-start.1
  2.2 1.3 %convert_element_type.17.w_ref = f32[4,1024]{1,0:T(4,128)} convert(bf16[4,1024]{1,0:T(4,128)(2,1)} %param.10) | non-fusion elementwise | flops 4096 | bytes 24576 | tf_op jit(solution)/shard_map/convert_element_type | solution.py:347
  3.6 0.1 mul.69
  3.6 0.1 reduce_sum.12
  3.7 0.7 mul.70.log_ref
  4.4 0.7 fusion.1.prior_ref
  5.1 53.3 %fold.1 = (bf16[2048,1024]{1,0:T(8,128)(2,1)}, bf16[2048,1024]{1,0:T(8,128)(2,1)}, bf16[2048,1024]{1,0:T(8,128)(2,1)}, bf16[2048,1024]{1,0:T(8,128)(2,1)}, f32[8...) custom-call(bf16[2048,1024]{1,0:T(8,128)(2,1)} %all_ref.1, ...), custom_call_target="tpu_custom_call" | custom-call | flops 4831838208 | bytes 41943040 | tf_op jit(solution)/shard_map/fold/pallas_call | solution.py:407
  58.4 0.0 copy-done.1
  58.4 14.8 %shared.1 = (bf16[8,256,1024]{2,1,0:T(8,128)(2,1)}, f32[2048,256]{1,0:T(8,128)}) custom-call(bf16[2048,1024]{1,0:T(8,128)(2,1)} %g_ref.3, bf16[2048,1024]{1,0:T(8,128)(2,1)} %get-tuple-element.22.dg_ref, bf16[2048,1024]{1,0:T(8,128)(2,1)} %get-tuple-element.23.act_ref, bf16[2048,1024]{1,0:T(8,128)(2,1)} %get-tuple-element.24.da_ref, ...), custom_call_target="tpu_custom_call" | custom-call | flops 4294967296 | bytes 29360128 | tf_op jit(solution)/shard_map/shared/pallas_call | solution.py:460
  73.1 0.0 copy-start
  73.2 1.8 %slice_select_fusion = f32[1024,256]{1,0:T(8,128)S(1)} fusion(f32[2048,256]{1,0:T(8,128)} %get-tuple-element.31, pred[]{:T(512)S(6)} %eq.7), kind=kLoop, calls=%fused_computation.9 | loop fusion | flops 262144 | bytes 3145729 | tf_op jit(solution)/shard_map/jit(_where)/select_n | solution.py:323
  75.0 0.1 collective-permute-start
  75.1 2.6 %collective-permute-done = f32[1024,256]{1,0:T(8,128)S(1)} collective-permute-done((f32[1024,256]{1,0:T(8,128)S(1)}, f32[1024,256]{1,0:T(8,128)S(1)}, u32[]{:S(2)}, u32[]{:S(2)}) %collective-permute-start) | collective-permute-done | bytes 1048608 | tf_op jit(solution)/shard_map/ppermute | solution.py:316
  77.7 0.0 copy-done
  77.7 0.3 select_add_fusion
  78.0 1.6 %collective-permute-start.1 = (bf16[1024,256]{1,0:T(8,128)(2,1)S(1)}, bf16[1024,256]{1,0:T(8,128)(2,1)S(1)}, u32[]{:S(2)}, u32[]{:S(2)}) collective-permute-start(bf16[1024,256]{1,0:T(8,128)(2,1)S(1)} %select_add_fusion), channel_id=1, source_target_pairs={{0,2},{1,3},{2,0},{3,1},{4,6},{5,7},{6,4},{7,5},{8,10},{9,11},{10,... | collective-permute-start | bytes 1572872 | tf_op jit(solution)/shard_map/ppermute | solution.py:316
  79.6 0.0 copy-start.2
  79.6 13.8 %inputs.1 = (f32[2048,1024]{1,0:T(8,128)}, f32[8,1024]{1,0:T(8,128)}) custom-call(bf16[2048,128]{1,0:T(8,128)(2,1)} %b_ref.3, f32[4,1024]{1,0:T(4,128)} %convert_element_type.17.w_ref, f32[8,1,1024]{2,1,0:T(1,128)} %copy-done.1, bf16[8,256,1024]{2,1,0:T(8,128)(2,1)} %get-tuple-element.33.pair_ref, bf16[2048,1024]{1,0:T(8,128)(2,1)} %get-tuple-element.34.ga_ref, ...), custom_call_target="tpu_custom_call" | custom-call | flops 1073741824 | bytes 20971520 | tf_op jit(solution)/shard_map/inputs/pallas_call | solution.py:483
  93.3 0.0 collective-permute-done.1
  93.3 0.1 convert_add_fusion
  93.4 0.1 collective-permute-start.3
  93.5 1.3 %collective-permute-start.2 = (f32[8,1024]{1,0:T(8,128)}, f32[8,1024]{1,0:T(8,128)S(1)}, u32[]{:S(2)}, u32[]{:S(2)}) collective-permute-start(f32[8,1024]{1,0:T(8,128)} %get-tuple-element.39), channel_id=1, source_target_pairs={{4,0},{8,4},{12,8},{16,12},{20,16},{24,20},{28,24},{5,1},{9,5},{13... | collective-permute-start | bytes 98312 | tf_op jit(solution)/shard_map/ppermute | solution.py:310
  94.8 5.3 %collective-permute-done.2 = f32[8,1024]{1,0:T(8,128)S(1)} collective-permute-done((f32[8,1024]{1,0:T(8,128)}, f32[8,1024]{1,0:T(8,128)S(1)}, u32[]{:S(2)}, u32[]{:S(2)}) %collective-permute-start.2) | collective-permute-done | bytes 32800 | tf_op jit(solution)/shard_map/ppermute | solution.py:310
  100.1 0.0 copy-done.2
  100.1 1.4 %fusion.4 = f32[2048,1024]{1,0:T(8,128)} fusion(f32[2048,1024]{1,0:T(8,128)} %get-tuple-element.36, f32[1,1024]{1,0:T(1,128)S(1)} %get-tuple-element.46, f32[1,1024]{1,0:T(1,128)S(1)} %get-tuple-element.47, f32[1,1024]{1,0:T(1,128)S(1)} %get-tuple-element.45), kind=kLoop, calls=%fused_computation.14 | loop fusion | flops 57344 | bytes 77824 | tf_op jit(solution)/shard_map/dynamic_update_slice | solution.py:507
  101.5 0.0 collective-permute-done.3
  101.5 0.1 broadcast_select_fusion
  101.7 1.5 %pad_maximum_fusion = (f32[2048,128]{1,0:T(8,128)}, f32[2048,128]{1,0:T(8,128)}) fusion(f32[1024,256]{1,0:T(8,128)S(1)} %get-tuple-element.43, f32[1024,256]{1,0:T(8,128)S(1)} %get-tuple-element.44), kind=kLoop, calls=%fused_computation.6 | loop fusion | flops 524288 | bytes 4194304 | tf_op jit(solution)/shard_map/concatenate | solution.py:338
  (2 shorter events, 0.0 us)
Async XLA Ops:
  2.2 56.1 %copy-start.1 = (f32[8,1,1024]{2,1,0:T(1,128)}, f32[8,1,1024]{2,1,0:T(1,128)S(1)}, u32[]{:S(2)}) copy-start(f32[8,1,1024]{2,1,0:T(1,128)S(1)} %broadcast_in_dim_reshape.3.lr_ref) | copy-start | bytes 98308
  73.1 4.6 %copy-start = (f32[2048,256]{1,0:T(8,128)S(1)}, f32[2048,256]{1,0:T(8,128)}, u32[]{:S(2)}) copy-start(f32[2048,256]{1,0:T(8,128)} %get-tuple-element.31) | copy-start | bytes 6291460
  75.0 2.7 %collective-permute-start = (f32[1024,256]{1,0:T(8,128)S(1)}, f32[1024,256]{1,0:T(8,128)S(1)}, u32[]{:S(2)}, u32[]{:S(2)}) collective-permute-start(f32[1024,256]{1,0:T(8,128)S(1)} %slice_select_fusion), channel_id=1, source_target_pairs={{0,1},{1,0},{2,3},{3,2},{4,5},{5,4},{6,7},{7,6},{8,9},{9,8},{10,11... | collective-permute-start | bytes 3145736 | tf_op jit(solution)/shard_map/ppermute | solution.py:316
  78.0 15.4 %collective-permute-start.1 = (bf16[1024,256]{1,0:T(8,128)(2,1)S(1)}, bf16[1024,256]{1,0:T(8,128)(2,1)S(1)}, u32[]{:S(2)}, u32[]{:S(2)}) collective-permute-start(bf16[1024,256]{1,0:T(8,128)(2,1)S(1)} %select_add_fusion), channel_id=1, source_target_pairs={{0,2},{1,3},{2,0},{3,1},{4,6},{5,7},{6,4},{7,5},{8,10},{9,11},{10,... | collective-permute-start | bytes 1572872 | tf_op jit(solution)/shard_map/ppermute | solution.py:316
  79.6 20.5 %copy-start.2 = (f32[4,1024]{1,0:T(4,128)S(1)}, f32[4,1024]{1,0:T(4,128)}, u32[]{:S(2)}) copy-start(f32[4,1024]{1,0:T(4,128)} %convert_element_type.17.w_ref) | copy-start | bytes 49156
  93.4 8.1 %collective-permute-start.3 = (f32[1024,256]{1,0:T(8,128)S(1)}, f32[1024,256]{1,0:T(8,128)S(1)}, u32[]{:S(2)}, u32[]{:S(2)}) collective-permute-start(f32[1024,256]{1,0:T(8,128)S(1)} %convert_add_fusion), channel_id=1, source_target_pairs={{0,1},{1,0},{2,3},{3,2},{4,5},{5,4},{6,7},{7,6},{8,9},{9,8},{10,11... | collective-permute-start | bytes 3145736 | tf_op jit(solution)/shard_map/ppermute | solution.py:316
  93.5 6.6 %collective-permute-start.2 = (f32[8,1024]{1,0:T(8,128)}, f32[8,1024]{1,0:T(8,128)S(1)}, u32[]{:S(2)}, u32[]{:S(2)}) collective-permute-start(f32[8,1024]{1,0:T(8,128)} %get-tuple-element.39), channel_id=1, source_target_pairs={{4,0},{8,4},{12,8},{16,12},{20,16},{24,20},{28,24},{5,1},{9,5},{13... | collective-permute-start | bytes 98312 | tf_op jit(solution)/shard_map/ppermute | solution.py:310

commit v4 on v3

--- a/solution.py
+++ b/solution.py
@@ -30,10 +30,13 @@
     return v
 
 
-def decays(lr, span):
+PIECE = 32
+
+
+def decays(lr, span, middle):
     width = lr.shape[1]
     rows = lax.broadcasted_iota(jnp.int32, (8, width), 0)
-    held = jnp.exp((rows - span // 2).astype(F32) * lr)
+    held = jnp.exp((rows - middle).astype(F32) * lr)
     length = 8
     while length < span:
         held = jnp.concatenate([held, held * jnp.exp(length * lr)], axis=0)
@@ -174,28 +177,30 @@
         xs[HALO : HALO + rows] = x_ref[...].astype(F32)
         for q in range(rows // span):
             at = q * span
-            here = slice(at, at + span)
             place = pl.multiple_of(part * rows + at, span)
             lr = lr_ref[pl.ds(part * (rows // span) + q, 1)]
             b = b_ref[pl.ds(place, span)].T
             c = c_ref[pl.ds(place, span)].T
-            v = preact_of(xs, w_ref, at, span)
-            squashed = 0.5 + 0.5 * jnp.tanh(0.5 * v)
-            full = v * squashed
-            slope_ref[here] = (squashed + full * (1.0 - squashed) - 0.5).astype(BF16)
-            a = full.astype(BF16)
-            act_ref[here] = a
-            af = a.astype(F32)
-            more = af * (decays(-lr, span) - 1.0)
-            da = more.astype(BF16)
-            da_ref[here] = da
-            ab[n, pl.ds(place, span)] = (af + more).astype(BF16)
-            g = g_ref[here]
-            gf = g.astype(F32)
-            more = gf * (decays(lr, span) - 1.0)
-            dg = more.astype(BF16)
-            dg_ref[here] = dg
-            gs[n, pl.ds(place, span)] = (gf + more).astype(BF16)
+            up, down_by = decays(lr, PIECE, half), decays(-lr, PIECE, half)
+            for first in range(0, span, PIECE):
+                here = slice(at + first, at + first + PIECE)
+                there = pl.ds(place + first, PIECE)
+                v = preact_of(xs, w_ref, at + first, PIECE)
+                squashed = 0.5 + 0.5 * jnp.tanh(0.5 * v)
+                full = v * squashed
+                slope_ref[here] = (squashed + full * (1.0 - squashed) - 0.5).astype(BF16)
+                a = full.astype(BF16)
+                act_ref[here] = a
+                af = a.astype(F32)
+                more = af * (down_by * jnp.exp(-first * lr) - 1.0)
+                da_ref[here] = more.astype(BF16)
+                ab[n, there] = (af + more).astype(BF16)
+                gf = g_ref[here].astype(F32)
+                more = gf * (up * jnp.exp(first * lr) - 1.0)
+                dg_ref[here] = more.astype(BF16)
+                gs[n, there] = (gf + more).astype(BF16)
+            here = slice(at, at + span)
+            a, da, g, dg = act_ref[here], da_ref[here], g_ref[here], dg_ref[here]
             fresh_state = jnp.exp((half - 1.0) * lr) * (mm(b, a, 1, 0) + mm(b, da, 1, 0))
             fresh_grad = jnp.exp((half + 1.0) * lr) * (mm(c, g, 1, 0) + mm(c, dg, 1, 0))
             state = held[0, n]
@@ -297,7 +302,7 @@
     for cols in chunks_of(channels):
         grad_act = mm(twice, pair_ref[0, :, cols], 1, 0) + ga_ref[:, cols].astype(F32)
         slope = slope_ref[:, cols].astype(F32) + 0.5
-        gp[0:span, cols] = grad_act * decays(-lr_ref[0, 0:1, cols], span) * slope
+        gp[0:span, cols] = grad_act * decays(-lr_ref[0, 0:1, cols], span, span // 2) * slope
         out = w_ref[0:1, cols] * gp[3 : 3 + span, cols]
         for k in range(1, 4):
             out = out + w_ref[k : k + 1, cols] * gp[3 - k : 3 - k + span, cols]
@@ -351,7 +356,7 @@
     own_log = span * jnp.sum(wide, axis=0, keepdims=True)
     lr = wide[:, None]
     params = pltpu.CompilerParams(
-        vmem_limit_bytes=60 << 20, dimension_semantics=("arbitrary",)
+        vmem_limit_bytes=48 << 20, dimension_semantics=("arbitrary",)
     )
     on = lambda t: t
     back = lambda t: spans - 1 - t

time: 104 us -> 103 us (level)
  local copies, waits for them, and re-layouts: 1.74 us -> 6.26 us
  Pallas kernels: 81.8 us -> 79 us
  other arithmetic: 7.87 us -> 5.56 us
    unnamed x6 -> x14, local copies, waits for them, and re-layouts: 0.02 us -> 4.54 us
    pallas_call x1, Pallas kernels: 14.8 us -> 12.8 us  [body(): pl.pallas_call(shared_kernel, grid=(spans,), in_specs=[tile(back, channel...]
    select_n x1, other arithmetic: 1.82 us -> 0.14 us  [half_sums(): jnp.where(odd, low, high)]
    pallas_call x1, Pallas kernels: 13.8 us -> 12.5 us  [body(): pl.pallas_call(input_kernel, grid=(spans,), in_specs=[tile(back, states),...]
  transfers between devices with their start and end apart: 4 -> 4, of which waited for: 2 -> 2; matrix products, arithmetic and copies ran while one was open for 1% -> 1% of each run, Pallas kernels for 13% -> 12%
where the time goes in v4:
time: 103 us; the launch traced here: 102 us
  Pallas kernels  79 us (77%)
  waiting for transfers between devices  7.47 us (7%)
  local copies, waits for them, and re-layouts  6.26 us (6%)
  other arithmetic  5.56 us (5%)
  starting transfers between devices  3.02 us (3%)
    pallas_call x1, Pallas kernels, body(): pl.pallas_call(functools.partial(fold_kernel, length, rounds, 'seq', span...  53.7 us
    pallas_call x1, Pallas kernels, body(): pl.pallas_call(shared_kernel, grid=(spans,), in_specs=[tile(back, channel...  12.8 us
    pallas_call x1, Pallas kernels, body(): pl.pallas_call(input_kernel, grid=(spans,), in_specs=[tile(back, states),...  12.5 us
    ppermute x1, waiting for transfers between devices, shifted(): lax.ppermute(array, axis, [(i, i + by) for i in range(length) if 0 <= i +...  4.82 us
    unnamed x14, local copies, waits for them, and re-layouts  4.54 us
    ppermute x3, waiting for transfers between devices, swapped(): lax.ppermute(array, axis, [(i, i ^ flip) for i in range(lax.axis_size(axi...  2.65 us
  transfers between devices with their start and end apart: 4, of which 2 were waited for; matrix products, arithmetic and copies ran while one was open for 1% of the time, Pallas kernels for 12%

profile of v4, /device:TPU:0, one launch (start us, length us, event | category | flops | bytes accessed | tf_op | source)
XLA Modules:
  0.0 102.1 jit_solution(464834574827622680)
XLA Ops:
  0.6 0.7 fusion.7
  1.3 0.1 broadcast_in_dim.2
  1.4 0.7 reshape.57.lr_ref
  2.1 0.1 broadcast_in_dim_reshape.3.lr_ref
  2.2 1.3 %convert_element_type.17.w_ref = f32[4,1024]{1,0:T(4,128)} convert(bf16[4,1024]{1,0:T(4,128)(2,1)} %param.10) | non-fusion elementwise | flops 4096 | bytes 24576 | tf_op jit(solution)/shard_map/convert_element_type | solution.py:352
  3.5 0.1 mul.69
  3.6 0.1 reduce_sum.12
  3.7 0.7 mul.70.log_ref
  4.4 0.1 fusion.1.prior_ref
  4.5 53.7 %fold.1 = (bf16[2048,1024]{1,0:T(8,128)(2,1)}, bf16[2048,1024]{1,0:T(8,128)(2,1)}, bf16[2048,1024]{1,0:T(8,128)(2,1)}, bf16[2048,1024]{1,0:T(8,128)(2,1)}, f32[8...) custom-call(bf16[2048,1024]{1,0:T(8,128)(2,1)} %all_ref.1, ...), custom_call_target="tpu_custom_call" | custom-call | flops 4831838208 | bytes 41943040 | tf_op jit(solution)/shard_map/fold/pallas_call | solution.py:412
  58.2 1.2 %copy-done.1 = f32[2048,128]{1,0:T(8,128)S(1)} copy-done((f32[2048,128]{1,0:T(8,128)S(1)}, f32[2048,128]{1,0:T(8,128)}, u32[]{:S(2)}) %copy-start.1) | copy-done | bytes 1048600
  59.4 1.2 %copy-done.2 = f32[2048,128]{1,0:T(8,128)S(1)} copy-done((f32[2048,128]{1,0:T(8,128)S(1)}, f32[2048,128]{1,0:T(8,128)}, u32[]{:S(2)}) %copy-start.2) | copy-done | bytes 1048600
  60.7 1.0 %copy-done.3 = f32[4,128,256]{2,1,0:T(8,128)S(1)} copy-done((f32[4,128,256]{2,1,0:T(8,128)S(1)}, f32[4,128,256]{2,1,0:T(8,128)}, u32[]{:S(2)}) %copy-start.3) | copy-done | bytes 524312
  61.7 1.0 %copy-done.4 = f32[4,128,256]{2,1,0:T(8,128)S(1)} copy-done((f32[4,128,256]{2,1,0:T(8,128)S(1)}, f32[4,128,256]{2,1,0:T(8,128)}, u32[]{:S(2)}) %copy-start.4) | copy-done | bytes 524312
  62.7 12.8 %shared.1 = (bf16[8,256,1024]{2,1,0:T(8,128)(2,1)}, f32[2048,256]{1,0:T(8,128)S(1)}) custom-call(bf16[2048,1024]{1,0:T(8,128)(2,1)} %g_ref.3, bf16[2048,1024]{1,0:T(8,128)(2,1)} %get-tuple-element.22.dg_ref, bf16[2048,1024]{1,0:T(8,128)(2,1)} %get-tuple-element.23.act_ref, bf16[2048,1024]{1,0:T(8,128)(2,1)} %get-tuple-element.24.da_ref, ...), custom_call_target="tpu_custom_call" | custom-call | flops 4294967296 | bytes 29360128 | tf_op jit(solution)/shard_map/shared/pallas_call | solution.py:465
  75.5 0.0 copy-start.6
  75.6 0.1 slice_select_fusion
  75.7 0.1 collective-permute-start
  75.8 2.6 %collective-permute-done = f32[1024,256]{1,0:T(8,128)S(1)} collective-permute-done((f32[1024,256]{1,0:T(8,128)S(1)}, f32[1024,256]{1,0:T(8,128)S(1)}, u32[]{:S(2)}, u32[]{:S(2)}) %collective-permute-start) | collective-permute-done | bytes 1048608 | tf_op jit(solution)/shard_map/ppermute | solution.py:321
  78.4 0.2 select_add_fusion
  78.7 1.6 %collective-permute-start.1 = (bf16[1024,256]{1,0:T(8,128)(2,1)S(1)}, bf16[1024,256]{1,0:T(8,128)(2,1)S(1)}, u32[]{:S(2)}, u32[]{:S(2)}) collective-permute-start(bf16[1024,256]{1,0:T(8,128)(2,1)S(1)} %select_add_fusion), channel_id=1, source_target_pairs={{0,2},{1,3},{2,0},{3,1},{4,6},{5,7},{6,4},{7,5},{8,10},{9,11},{10,... | collective-permute-start | bytes 1572872 | tf_op jit(solution)/shard_map/ppermute | solution.py:321
  80.3 0.0 copy-done.5
  80.3 12.5 %inputs.1 = (f32[2048,1024]{1,0:T(8,128)}, f32[8,1024]{1,0:T(8,128)S(1)}) custom-call(bf16[2048,128]{1,0:T(8,128)(2,1)S(1)} %copy-done.5, f32[4,1024]{1,0:T(4,128)S(1)} %copy-done.6, f32[8,1,1024]{2,1,0:T(1,128)S(1)} %broadcast_in_dim_reshape.3.lr_ref, bf16[8,256,1024]{2,1,0:T(8,128)(2,1)S(1)} %copy-done, bf16[2048,1024]{1,0:T(8,128)(2,1)} %get-tuple-element.34.ga_ref, ...), custom_call_target="tpu_custom_call" | custom-call | flops 1073741824 | bytes 20971520 | tf_op jit(solution)/shard_map/inputs/pallas_call | solution.py:488
  92.8 0.0 collective-permute-done.1
  92.8 0.1 convert_add_fusion
  92.9 0.1 collective-permute-start.3
  93.0 1.3 %collective-permute-start.2 = (f32[8,1024]{1,0:T(8,128)S(1)}, f32[8,1024]{1,0:T(8,128)S(1)}, u32[]{:S(2)}, u32[]{:S(2)}) collective-permute-start(f32[8,1024]{1,0:T(8,128)S(1)} %get-tuple-element.39), channel_id=1, source_target_pairs={{4,0},{8,4},{12,8},{16,12},{20,16},{24,20},{28,24},{5,1},{9,5},{13... | collective-permute-start | bytes 98312 | tf_op jit(solution)/shard_map/ppermute | solution.py:315
  94.3 4.8 %collective-permute-done.2 = f32[8,1024]{1,0:T(8,128)S(1)} collective-permute-done((f32[8,1024]{1,0:T(8,128)S(1)}, f32[8,1024]{1,0:T(8,128)S(1)}, u32[]{:S(2)}, u32[]{:S(2)}) %collective-permute-start.2) | collective-permute-done | bytes 32800 | tf_op jit(solution)/shard_map/ppermute | solution.py:315
  99.1 1.4 %fusion.4 = f32[2048,1024]{1,0:T(8,128)} fusion(f32[2048,1024]{1,0:T(8,128)} %get-tuple-element.36, f32[1,1024]{1,0:T(1,128)S(1)} %get-tuple-element.46, f32[1,1024]{1,0:T(1,128)S(1)} %get-tuple-element.47, f32[1,1024]{1,0:T(1,128)S(1)} %get-tuple-element.45), kind=kLoop, calls=%fused_computation.14 | loop fusion | flops 57344 | bytes 77824 | tf_op jit(solution)/shard_map/dynamic_update_slice | solution.py:512
  100.5 0.0 collective-permute-done.3
  100.5 0.1 broadcast_select_fusion
  100.6 1.5 %pad_maximum_fusion = (f32[2048,128]{1,0:T(8,128)}, f32[2048,128]{1,0:T(8,128)}) fusion(f32[1024,256]{1,0:T(8,128)S(1)} %get-tuple-element.43, f32[1024,256]{1,0:T(8,128)S(1)} %get-tuple-element.44), kind=kLoop, calls=%fused_computation.6 | loop fusion | flops 524288 | bytes 4194304 | tf_op jit(solution)/shard_map/concatenate | solution.py:343
  (10 shorter events, 0.0 us)
Async XLA Ops:
  58.2 1.2 %copy-start.1 = (f32[2048,128]{1,0:T(8,128)S(1)}, f32[2048,128]{1,0:T(8,128)}, u32[]{:S(2)}) copy-start(f32[2048,128]{1,0:T(8,128)} %get-tuple-element.29.inner_b_ref) | copy-start | bytes 3145732
  59.4 1.2 %copy-start.2 = (f32[2048,128]{1,0:T(8,128)S(1)}, f32[2048,128]{1,0:T(8,128)}, u32[]{:S(2)}) copy-start(f32[2048,128]{1,0:T(8,128)} %get-tuple-element.30.inner_c_ref) | copy-start | bytes 3145732
  60.7 1.0 %copy-start.3 = (f32[4,128,256]{2,1,0:T(8,128)S(1)}, f32[4,128,256]{2,1,0:T(8,128)}, u32[]{:S(2)}) copy-start(f32[4,128,256]{2,1,0:T(8,128)} %get-tuple-element.27.entering_ref) | copy-start | bytes 1572868
  61.7 1.0 %copy-start.4 = (f32[4,128,256]{2,1,0:T(8,128)S(1)}, f32[4,128,256]{2,1,0:T(8,128)}, u32[]{:S(2)}) copy-start(f32[4,128,256]{2,1,0:T(8,128)} %get-tuple-element.28.arriving_ref) | copy-start | bytes 1572868
  75.5 4.7 %copy-start = (bf16[8,256,1024]{2,1,0:T(8,128)(2,1)S(1)}, bf16[8,256,1024]{2,1,0:T(8,128)(2,1)}, u32[]{:S(2)}) copy-start(bf16[8,256,1024]{2,1,0:T(8,128)(2,1)} %get-tuple-element.33.pair_ref) | copy-start | bytes 12582916
  75.5 4.7 %copy-start.5 = (bf16[2048,128]{1,0:T(8,128)(2,1)S(1)}, bf16[2048,128]{1,0:T(8,128)(2,1)}, u32[]{:S(2)}) copy-start(bf16[2048,128]{1,0:T(8,128)(2,1)} %b_ref.3) | copy-start | bytes 1572868
  75.5 4.7 %copy-start.6 = (f32[4,1024]{1,0:T(4,128)S(1)}, f32[4,1024]{1,0:T(4,128)}, u32[]{:S(2)}) copy-start(f32[4,1024]{1,0:T(4,128)} %convert_element_type.17.w_ref) | copy-start | bytes 49156
  75.7 2.7 %collective-permute-start = (f32[1024,256]{1,0:T(8,128)S(1)}, f32[1024,256]{1,0:T(8,128)S(1)}, u32[]{:S(2)}, u32[]{:S(2)}) collective-permute-start(f32[1024,256]{1,0:T(8,128)S(1)} %slice_select_fusion), channel_id=1, source_target_pairs={{0,1},{1,0},{2,3},{3,2},{4,5},{5,4},{6,7},{7,6},{8,9},{9,8},{10,11... | collective-permute-start | bytes 3145736 | tf_op jit(solution)/shard_map/ppermute | solution.py:321
  78.7 14.1 %collective-permute-start.1 = (bf16[1024,256]{1,0:T(8,128)(2,1)S(1)}, bf16[1024,256]{1,0:T(8,128)(2,1)S(1)}, u32[]{:S(2)}, u32[]{:S(2)}) collective-permute-start(bf16[1024,256]{1,0:T(8,128)(2,1)S(1)} %select_add_fusion), channel_id=1, source_target_pairs={{0,2},{1,3},{2,0},{3,1},{4,6},{5,7},{6,4},{7,5},{8,10},{9,11},{10,... | collective-permute-start | bytes 1572872 | tf_op jit(solution)/shard_map/ppermute | solution.py:321
  92.9 7.6 %collective-permute-start.3 = (f32[1024,256]{1,0:T(8,128)S(1)}, f32[1024,256]{1,0:T(8,128)S(1)}, u32[]{:S(2)}, u32[]{:S(2)}) collective-permute-start(f32[1024,256]{1,0:T(8,128)S(1)} %convert_add_fusion), channel_id=1, source_target_pairs={{0,1},{1,0},{2,3},{3,2},{4,5},{5,4},{6,7},{7,6},{8,9},{9,8},{10,11... | collective-permute-start | bytes 3145736 | tf_op jit(solution)/shard_map/ppermute | solution.py:321
  93.0 6.1 %collective-permute-start.2 = (f32[8,1024]{1,0:T(8,128)S(1)}, f32[8,1024]{1,0:T(8,128)S(1)}, u32[]{:S(2)}, u32[]{:S(2)}) collective-permute-start(f32[8,1024]{1,0:T(8,128)S(1)} %get-tuple-element.39), channel_id=1, source_target_pairs={{4,0},{8,4},{12,8},{16,12},{20,16},{24,20},{28,24},{5,1},{9,5},{13... | collective-permute-start | bytes 98312 | tf_op jit(solution)/shard_map/ppermute | solution.py:315
